TPU v7x, 32 devices: a whole 2x2x4 slice. The times are simulated.
32 devices in a mesh: shard: 2 (over y), ctx: 8 (over z, x), tp: 2 (over core).
Axes of the slice: x: 2, y: 2, z: 4, core: 2. Of those that a mesh axis runs over, the one named last changes fastest.
Arguments:
- tokens: bfloat16 [8192, 1024], P(('shard', 'ctx')), may hold values from -6 to 6
- cotangent: bfloat16 [8192, 1024], P(('shard', 'ctx')), may hold values from -6 to 6
- lengths: int32 [2, 4], P('shard'), may hold values from 1 to 4093, as said below
- g_attn: bfloat16 [1024], P('shard'), may hold values from 0.099609375 to 1.8984375
- w_qkv: bfloat16 [1024, 3, 1024], P('shard', None, 'tp'), may hold values from -0.1875 to 0.1875
- w_attn_out: bfloat16 [1024, 1024], P('tp', 'shard'), may hold values from -6 to 6
- g_mlp: bfloat16 [1024], P('shard'), may hold values from 0.099609375 to 1.8984375
- w_in: bfloat16 [1024, 2, 2624], P('shard', None, 'tp'), may hold values from -0.1875 to 0.1875
- w_mlp_out: bfloat16 [2624, 1024], P('tp', 'shard'), may hold values from -0.125 to 0.125
Outputs:
- output: bfloat16 [8192, 1024], P(('shard', 'ctx'))
- grad_tokens: bfloat16 [8192, 1024], P(('shard', 'ctx'))
- grad_g_attn: float32 [1024], P('shard')
- grad_w_qkv: float32 [1024, 3, 1024], P('shard', None, 'tp')
- grad_w_attn_out: float32 [1024, 1024], P('tp', 'shard')
- grad_g_mlp: float32 [1024], P('shard')
- grad_w_in: float32 [1024, 2, 2624], P('shard', None, 'tp')
- grad_w_mlp_out: float32 [2624, 1024], P('tp', 'shard')
Inputs may be any that keep to these rules, and one draw needn't show every extreme that they name: `lengths`: each row sums to 4096. In every group one sequence, at a place drawn anew, starts within the first 512 tokens and ends within the last 512; the longest sequence of all groups has 4093 tokens.
All inputs are finite; a program needn't handle non-finite values.
Results may differ from a plain program's by a relative error of at most 0.024.
Values may be sent and summed in bfloat16 or wider, within the bound.
A program may use at most 128 MiB of HBM per device.

v0:
```python
import math

import jax
import jax.numpy as jnp
from jax import lax
from jax.sharding import PartitionSpec as P

HD = 64


EPSILON = 1e-05
ROPE_BASE = 160000.0
MASKED = -1e30


def shifted(block, axis, distance):
    devices = range(lax.axis_size(axis))
    route = [((i - distance) % len(devices), i) for i in devices]
    return lax.ppermute(block, axis, route)


def layer_norm(values, norm_gain):
    average = jnp.mean(values, axis=-1, keepdims=True)
    centred = values - average
    spread = jnp.mean(centred * centred, axis=-1, keepdims=True)
    return centred * lax.rsqrt(spread + EPSILON) * norm_gain


def rotate(values, cos_table, sin_table):
    half_size = values.shape[-1] // 2
    front_half = values[..., :half_size]
    back_half = values[..., half_size:]
    cos_rows = cos_table[:, None, :]
    sin_rows = sin_table[:, None, :]
    return jnp.concatenate(
        [
            front_half * cos_rows - back_half * sin_rows,
            back_half * cos_rows + front_half * sin_rows,
        ],
        axis=-1,
    )


def rope_tables(places, head_size):
    half_size = head_size // 2
    powers = jnp.arange(half_size, dtype=jnp.float32) * (-2.0 * math.log(ROPE_BASE) / head_size)
    angles = places.astype(jnp.float32)[:, None] * jnp.exp(powers)[None, :]
    return (jnp.cos(angles), jnp.sin(angles))


def positions_of(seq_lengths, places):
    seq_count = seq_lengths.shape[0]
    seq_ends = jnp.cumsum(seq_lengths)
    seq_starts = seq_ends - seq_lengths
    segment = jnp.sum((places[:, None] >= seq_ends[None, :]).astype(jnp.int32), axis=1)
    chosen = segment[:, None] == jnp.arange(seq_count, dtype=jnp.int32)[None, :]
    seq_first = jnp.sum(jnp.where(chosen, seq_starts[None, :], 0), axis=1)
    return (segment, places - seq_first)


def geglu(lifted):
    return jax.nn.gelu(lifted[:, 0], approximate=False) * lifted[:, 1]


def split_block(kv_block, head_count):
    key_count = kv_block.shape[1]
    return (
        kv_block[0].reshape(key_count, head_count, -1),
        kv_block[1].reshape(key_count, head_count, -1),
    )


def masked_scores(queries, key_rows, seg_query, seg_keys, scaling):
    scores = (
        jnp.einsum("qhd,khd->hqk", queries, key_rows, preferred_element_type=jnp.float32) * scaling
    )
    same_seg = (seg_query[:, None] == seg_keys[None, :])[None]
    return (jnp.where(same_seg, scores, MASKED), same_seg)


def forward_step(soft_state, kv_block, seg_keys, queries, seg_query, scaling):
    maxima, totals, running = soft_state
    key_rows, values = split_block(kv_block, queries.shape[1])
    scores, same_seg = masked_scores(queries, key_rows, seg_query, seg_keys, scaling)
    new_max = jnp.maximum(maxima, jnp.max(scores, axis=-1))
    weights = jnp.where(same_seg, jnp.exp(scores - new_max[..., None]), 0.0)
    factor = jnp.exp(maxima - new_max)
    totals = totals * factor + jnp.sum(weights, axis=-1)
    update = jnp.einsum(
        "hqk,khd->hqd", weights.astype(jnp.bfloat16), values, preferred_element_type=jnp.float32
    )
    return (new_max, totals, running * factor[..., None] + update)


def backward_step(kv_block, seg_keys, queries, seg_query, grad_heads, log_sums, row_delta, scaling):
    key_rows, values = split_block(kv_block, queries.shape[1])
    scores, same_seg = masked_scores(queries, key_rows, seg_query, seg_keys, scaling)
    weights = jnp.where(same_seg, jnp.exp(scores - log_sums[..., None]), 0.0)
    grad_weights = jnp.einsum(
        "qhd,khd->hqk", grad_heads, values, preferred_element_type=jnp.float32
    )
    grad_scores = (weights * (grad_weights - row_delta[..., None])).astype(jnp.bfloat16)
    grad_query = (
        jnp.einsum("hqk,khd->qhd", grad_scores, key_rows, preferred_element_type=jnp.float32)
        * scaling
    )
    grad_keys = (
        jnp.einsum("hqk,qhd->khd", grad_scores, queries, preferred_element_type=jnp.float32)
        * scaling
    )
    grad_values = jnp.einsum(
        "hqk,qhd->khd", weights.astype(jnp.bfloat16), grad_heads, preferred_element_type=jnp.float32
    )
    key_count = key_rows.shape[0]
    return (
        grad_query,
        jnp.stack([grad_keys.reshape(key_count, -1), grad_values.reshape(key_count, -1)]),
    )


def shards(tokens, cotangent, lengths, g_attn, w_qkv, w_attn_out, g_mlp, w_in, w_mlp_out):
    tok_rows = tokens.shape[0]
    ctx_size = lax.axis_size("ctx")
    ctx_place = lax.axis_index("ctx")
    seq_lengths = lengths[0]
    row_index = jnp.arange(tok_rows, dtype=jnp.int32)
    segment_local, inside = positions_of(seq_lengths, ctx_place * tok_rows + row_index)
    cos_table, sin_table = rope_tables(inside, HD)
    scaling = 1.0 / math.sqrt(HD)

    def segments_from(source):
        return positions_of(seq_lengths, source * tok_rows + row_index)[0]

    attn_gain, qkv_full, out_full = (
        lax.all_gather(g_attn, "shard", axis=0, tiled=True),
        lax.all_gather(w_qkv, "shard", axis=0, tiled=True),
        lax.all_gather(w_attn_out, "shard", axis=1, tiled=True),
    )
    residual = tokens.astype(jnp.float32)
    normed_one, norm_one_back = jax.vjp(layer_norm, residual, attn_gain.astype(jnp.float32))
    hidden_one = normed_one.astype(jnp.bfloat16)
    projected = jnp.einsum("td,dcn->tcn", hidden_one, qkv_full, preferred_element_type=jnp.float32)
    local_width = projected.shape[2]
    head_count = local_width // HD
    split_heads = projected.reshape(tok_rows, 3, head_count, HD)
    queries = rotate(split_heads[:, 0], cos_table, sin_table).astype(jnp.bfloat16)
    key_rows = rotate(split_heads[:, 1], cos_table, sin_table).astype(jnp.bfloat16)
    values = split_heads[:, 2].astype(jnp.bfloat16)
    key_vals = jnp.stack(
        [key_rows.reshape(tok_rows, local_width), values.reshape(tok_rows, local_width)]
    )

    def attend(soft_state, kv_block, source):
        return forward_step(
            soft_state, kv_block, segments_from(source), queries, segment_local, scaling
        )

    start_state = (
        jnp.full((head_count, tok_rows), MASKED, jnp.float32),
        jnp.zeros((head_count, tok_rows), jnp.float32),
        jnp.zeros((head_count, tok_rows, HD), jnp.float32),
    )
    first_state = attend(start_state, key_vals, ctx_place)

    def pass_forward(step_index, carry):
        moving, soft_state = carry
        moving = shifted(moving, "ctx", 1)
        source = (ctx_place - step_index) % ctx_size
        return (moving, attend(soft_state, moving, source))

    _, soft_state = lax.fori_loop(1, ctx_size, pass_forward, (key_vals, first_state))
    maxima, totals, running = soft_state
    attended = running / totals[..., None]
    log_sums = maxima + jnp.log(totals)
    attn_low = (
        jnp.transpose(attended, (1, 0, 2)).reshape(tok_rows, local_width).astype(jnp.bfloat16)
    )
    attn_part = jnp.dot(attn_low, out_full, preferred_element_type=jnp.float32)
    middle = residual + lax.psum(attn_part.astype(jnp.bfloat16), "tp").astype(jnp.float32)
    mlp_gain, in_full, down_full = (
        lax.all_gather(g_mlp, "shard", axis=0, tiled=True),
        lax.all_gather(w_in, "shard", axis=0, tiled=True),
        lax.all_gather(w_mlp_out, "shard", axis=1, tiled=True),
    )
    normed_two, norm_two_back = jax.vjp(layer_norm, middle, mlp_gain.astype(jnp.float32))
    hidden_two = normed_two.astype(jnp.bfloat16)
    lifted = jnp.einsum("td,dcf->tcf", hidden_two, in_full, preferred_element_type=jnp.float32)
    mixed_f, geglu_back = jax.vjp(geglu, lifted)
    mixed_low = mixed_f.astype(jnp.bfloat16)
    mlp_part = jnp.dot(mixed_low, down_full, preferred_element_type=jnp.float32)
    output = (middle + lax.psum(mlp_part.astype(jnp.bfloat16), "tp").astype(jnp.float32)).astype(
        jnp.bfloat16
    )
    grad_down = jnp.einsum("tf,td->fd", mixed_low, cotangent, preferred_element_type=jnp.float32)
    grad_mixed = jnp.einsum("td,fd->tf", cotangent, down_full, preferred_element_type=jnp.float32)
    (grad_lifted,) = geglu_back(grad_mixed)
    lifted_low = grad_lifted.astype(jnp.bfloat16)
    grad_in = jnp.einsum("td,tcf->dcf", hidden_two, lifted_low, preferred_element_type=jnp.float32)
    hidden_two_part = jnp.einsum(
        "tcf,dcf->td", lifted_low, in_full, preferred_element_type=jnp.float32
    )
    grad_hidden_two = lax.psum(hidden_two_part.astype(jnp.bfloat16), "tp").astype(jnp.float32)
    grad_middle_norm, grad_mlp_gain = norm_two_back(grad_hidden_two)
    grad_middle = cotangent.astype(jnp.float32) + grad_middle_norm
    grad_branch = grad_middle.astype(jnp.bfloat16)
    grad_attn_out = jnp.einsum(
        "tn,td->nd", attn_low, grad_branch, preferred_element_type=jnp.float32
    )
    grad_attended = jnp.einsum(
        "td,nd->tn", grad_branch, out_full, preferred_element_type=jnp.float32
    ).astype(jnp.bfloat16)
    grad_heads = grad_attended.reshape(tok_rows, head_count, HD)
    row_delta = jnp.sum(
        jnp.transpose(grad_heads.astype(jnp.float32), (1, 0, 2)) * attended, axis=-1
    )

    def back_block(kv_block, source):
        return backward_step(
            kv_block,
            segments_from(source),
            queries,
            segment_local,
            grad_heads,
            log_sums,
            row_delta,
            scaling,
        )

    grad_query, grad_block = back_block(key_vals, ctx_place)

    def pass_backward(step_index, carry):
        moving, carried, grad_sofar = carry
        moving = shifted(moving, "ctx", 1)
        carried = shifted(carried.astype(jnp.bfloat16), "ctx", 1).astype(carried.dtype)
        source = (ctx_place - step_index) % ctx_size
        more_query, more_block = back_block(moving, source)
        return (moving, carried + more_block, grad_sofar + more_query)

    _, carried, grad_query = lax.fori_loop(
        1, ctx_size, pass_backward, (key_vals, grad_block, grad_query)
    )
    grad_keyvals = shifted(carried.astype(jnp.bfloat16), "ctx", 1).astype(carried.dtype)
    grad_keys = grad_keyvals[0].reshape(tok_rows, head_count, HD)
    grad_values = grad_keyvals[1].reshape(tok_rows, head_count, HD)
    grad_projected = jnp.stack(
        [
            rotate(grad_query, cos_table, -sin_table),
            rotate(grad_keys, cos_table, -sin_table),
            grad_values,
        ],
        axis=1,
    )
    grad_projected = grad_projected.reshape(tok_rows, 3, local_width).astype(jnp.bfloat16)
    grad_qkv = jnp.einsum(
        "td,tcn->dcn", hidden_one, grad_projected, preferred_element_type=jnp.float32
    )
    hidden_one_part = jnp.einsum(
        "tcn,dcn->td", grad_projected, qkv_full, preferred_element_type=jnp.float32
    )
    grad_hidden_one = lax.psum(hidden_one_part.astype(jnp.bfloat16), "tp").astype(jnp.float32)
    grad_input_norm, grad_attn_gain = norm_one_back(grad_hidden_one)
    grad_tokens = (grad_middle + grad_input_norm).astype(jnp.bfloat16)
    sharded = (
        lax.psum_scatter(
            grad_attn_gain.astype(jnp.bfloat16), "shard", scatter_dimension=0, tiled=True
        ).astype(jnp.float32),
        lax.psum_scatter(
            grad_qkv.astype(jnp.bfloat16), "shard", scatter_dimension=0, tiled=True
        ).astype(jnp.float32),
        lax.psum_scatter(
            grad_attn_out.astype(jnp.bfloat16), "shard", scatter_dimension=1, tiled=True
        ).astype(jnp.float32),
        lax.psum_scatter(
            grad_mlp_gain.astype(jnp.bfloat16), "shard", scatter_dimension=0, tiled=True
        ).astype(jnp.float32),
        lax.psum_scatter(
            grad_in.astype(jnp.bfloat16), "shard", scatter_dimension=0, tiled=True
        ).astype(jnp.float32),
        lax.psum_scatter(
            grad_down.astype(jnp.bfloat16), "shard", scatter_dimension=1, tiled=True
        ).astype(jnp.float32),
    )
    summed = (
        lax.psum(sharded[0].astype(jnp.bfloat16), "ctx").astype(jnp.float32),
        lax.psum(sharded[1].astype(jnp.bfloat16), "ctx").astype(jnp.float32),
        lax.psum(sharded[2].astype(jnp.bfloat16), "ctx").astype(jnp.float32),
        lax.psum(sharded[3].astype(jnp.bfloat16), "ctx").astype(jnp.float32),
        lax.psum(sharded[4].astype(jnp.bfloat16), "ctx").astype(jnp.float32),
        lax.psum(sharded[5].astype(jnp.bfloat16), "ctx").astype(jnp.float32),
    )
    return (output, grad_tokens, summed[0], summed[1], summed[2], summed[3], summed[4], summed[5])


def solution(mesh):
    return jax.shard_map(
        shards,
        mesh=mesh,
        in_specs=(
            P(("shard", "ctx"), None),
            P(("shard", "ctx"), None),
            P("shard", None),
            P("shard"),
            P("shard", None, "tp"),
            P("tp", "shard"),
            P("shard"),
            P("shard", None, "tp"),
            P("tp", "shard"),
        ),
        out_specs=(
            P(("shard", "ctx"), None),
            P(("shard", "ctx"), None),
            P("shard"),
            P("shard", None, "tp"),
            P("tp", "shard"),
            P("shard"),
            P("shard", None, "tp"),
            P("tp", "shard"),
        ),
        check_vma=False,
    )
```

profile of v0, /device:TPU:0, one launch (start us, length us, event | category | flops | bytes accessed | tf_op | source)
XLA Modules:
  0.0 1220.7 jit_solution(8811887246230221731)
XLA Ops:
  19.7 38.1 %all-gather.7.cloned.1.call-done = bf16[1024,3,512]{0,2,1:T(8,128)(2,1)} async-done(((bf16[512,3,512]{0,2,1:T(8,128)(2,1)}), bf16[1024,3,512]{0,2,1:T(8,128)(2,1)}) %all-gather.7.cloned.1.call-update) | async-done | bytes 3145744 | tf_op jit(solution)/shard_map/all_gather | solution.py:136
  72.1 227.4 %while.42 = (s32[]{:T(128)}, bf16[2,512,512]{1,2,0:T(8,128)(2,1)}, f32[8,512]{1,0:T(8,128)S(1)}, f32[8,512]{1,0:T(8,128)S(1)}, f32[8,512,64]{1,2,0:T(8,128)}, /*...) while((s32[]{:T(128)}, bf16[2,512,512]{1,2,0:T(8,128)(2,1)}, ...), condition=%wide.region_12.13_spmd.clone, body=%wide.region_8.12_spmd.clone.sunk | while | flops 564934656 | bytes 46934396 | solution.py:171
  73.9 26.0 %collective-permute-done = bf16[2,512,512]{1,2,0:T(8,128)(2,1)S(1)} collective-permute-done((bf16[2,512,512]{1,2,0:T(8,128)(2,1)}, bf16[2,512,512]{1,2,0:T(8,128)(2,1)S(1)}, u32[]{:S(2)}, u32[]{:S(2)}) %collective-permute-start) | collective-permute-done | bytes 1048608 | tf_op jit(solution)/shard_map/while/body/eval_jaxpr/ppermute | solution.py:19
  107.6 26.6 %collective-permute-done = bf16[2,512,512]{1,2,0:T(8,128)(2,1)S(1)} collective-permute-done((bf16[2,512,512]{1,2,0:T(8,128)(2,1)}, bf16[2,512,512]{1,2,0:T(8,128)(2,1)S(1)}, u32[]{:S(2)}, u32[]{:S(2)}) %collective-permute-start) | collective-permute-done | bytes 1048608 | tf_op jit(solution)/shard_map/while/body/eval_jaxpr/ppermute | solution.py:19
  141.9 25.7 %collective-permute-done = bf16[2,512,512]{1,2,0:T(8,128)(2,1)S(1)} collective-permute-done((bf16[2,512,512]{1,2,0:T(8,128)(2,1)}, bf16[2,512,512]{1,2,0:T(8,128)(2,1)S(1)}, u32[]{:S(2)}, u32[]{:S(2)}) %collective-permute-start) | collective-permute-done | bytes 1048608 | tf_op jit(solution)/shard_map/while/body/eval_jaxpr/ppermute | solution.py:19
  175.4 24.8 %collective-permute-done = bf16[2,512,512]{1,2,0:T(8,128)(2,1)S(1)} collective-permute-done((bf16[2,512,512]{1,2,0:T(8,128)(2,1)}, bf16[2,512,512]{1,2,0:T(8,128)(2,1)S(1)}, u32[]{:S(2)}, u32[]{:S(2)}) %collective-permute-start) | collective-permute-done | bytes 1048608 | tf_op jit(solution)/shard_map/while/body/eval_jaxpr/ppermute | solution.py:19
  207.9 23.9 %collective-permute-done = bf16[2,512,512]{1,2,0:T(8,128)(2,1)S(1)} collective-permute-done((bf16[2,512,512]{1,2,0:T(8,128)(2,1)}, bf16[2,512,512]{1,2,0:T(8,128)(2,1)S(1)}, u32[]{:S(2)}, u32[]{:S(2)}) %collective-permute-start) | collective-permute-done | bytes 1048608 | tf_op jit(solution)/shard_map/while/body/eval_jaxpr/ppermute | solution.py:19
  239.4 22.9 %collective-permute-done = bf16[2,512,512]{1,2,0:T(8,128)(2,1)S(1)} collective-permute-done((bf16[2,512,512]{1,2,0:T(8,128)(2,1)}, bf16[2,512,512]{1,2,0:T(8,128)(2,1)S(1)}, u32[]{:S(2)}, u32[]{:S(2)}) %collective-permute-start) | collective-permute-done | bytes 1048608 | tf_op jit(solution)/shard_map/while/body/eval_jaxpr/ppermute | solution.py:19
  270.1 22.0 %collective-permute-done = bf16[2,512,512]{1,2,0:T(8,128)(2,1)S(1)} collective-permute-done((bf16[2,512,512]{1,2,0:T(8,128)(2,1)}, bf16[2,512,512]{1,2,0:T(8,128)(2,1)S(1)}, u32[]{:S(2)}, u32[]{:S(2)}) %collective-permute-start) | collective-permute-done | bytes 1048608 | tf_op jit(solution)/shard_map/while/body/eval_jaxpr/ppermute | solution.py:19
  323.8 70.5 %all-gather.11.cloned.1.call-done = bf16[1024,2,1312]{0,2,1:T(8,128)(2,1)} async-done(((bf16[512,2,1312]{0,2,1:T(8,128)(2,1)}), bf16[1024,2,1312]{0,2,1:T(8,128)(2,1)}) %all-gather.11.cloned.1.call-update) | async-done | bytes 5373968 | tf_op jit(solution)/shard_map/all_gather | solution.py:182
  464.0 355.5 %while.43 = (s32[]{:T(128)}, bf16[2,512,512]{1,2,0:T(8,128)(2,1)}, bf16[2,512,512]{1,2,0:T(8,128)(2,1)}, f32[512,8,64]{0,2,1:T(8,128)}, s32[512]{0:T(512)S(1)}, ...) while((s32[]{:T(128)}, bf16[2,512,512]{1,2,0:T(8,128)(2,1)}, ...), condition=%wide.region_23.24_spmd.clone, body=%wide.region_21.23_spmd.clone.sunk | while | flops 1370494976 | bytes 73722320 | solution.py:239
  467.6 25.3 %collective-permute-done.1 = bf16[2,512,512]{1,2,0:T(8,128)(2,1)S(1)} collective-permute-done((bf16[2,512,512]{1,2,0:T(8,128)(2,1)}, bf16[2,512,512]{1,2,0:T(8,128)(2,1)S(1)}, u32[]{:S(2)}, u32[]{:S(2)}) %collective-permute-start.1) | collective-permute-done | bytes 1048608 | tf_op jit(solution)/shard_map/while/body/eval_jaxpr/ppermute | solution.py:19
  519.1 27.3 %collective-permute-done.1 = bf16[2,512,512]{1,2,0:T(8,128)(2,1)S(1)} collective-permute-done((bf16[2,512,512]{1,2,0:T(8,128)(2,1)}, bf16[2,512,512]{1,2,0:T(8,128)(2,1)S(1)}, u32[]{:S(2)}, u32[]{:S(2)}) %collective-permute-start.1) | collective-permute-done | bytes 1048608 | tf_op jit(solution)/shard_map/while/body/eval_jaxpr/ppermute | solution.py:19
  570.4 28.7 %collective-permute-done.1 = bf16[2,512,512]{1,2,0:T(8,128)(2,1)S(1)} collective-permute-done((bf16[2,512,512]{1,2,0:T(8,128)(2,1)}, bf16[2,512,512]{1,2,0:T(8,128)(2,1)S(1)}, u32[]{:S(2)}, u32[]{:S(2)}) %collective-permute-start.1) | collective-permute-done | bytes 1048608 | tf_op jit(solution)/shard_map/while/body/eval_jaxpr/ppermute | solution.py:19
  622.2 28.7 %collective-permute-done.1 = bf16[2,512,512]{1,2,0:T(8,128)(2,1)S(1)} collective-permute-done((bf16[2,512,512]{1,2,0:T(8,128)(2,1)}, bf16[2,512,512]{1,2,0:T(8,128)(2,1)S(1)}, u32[]{:S(2)}, u32[]{:S(2)}) %collective-permute-start.1) | collective-permute-done | bytes 1048608 | tf_op jit(solution)/shard_map/while/body/eval_jaxpr/ppermute | solution.py:19
  673.0 28.7 %collective-permute-done.1 = bf16[2,512,512]{1,2,0:T(8,128)(2,1)S(1)} collective-permute-done((bf16[2,512,512]{1,2,0:T(8,128)(2,1)}, bf16[2,512,512]{1,2,0:T(8,128)(2,1)S(1)}, u32[]{:S(2)}, u32[]{:S(2)}) %collective-permute-start.1) | collective-permute-done | bytes 1048608 | tf_op jit(solution)/shard_map/while/body/eval_jaxpr/ppermute | solution.py:19
  722.9 28.7 %collective-permute-done.1 = bf16[2,512,512]{1,2,0:T(8,128)(2,1)S(1)} collective-permute-done((bf16[2,512,512]{1,2,0:T(8,128)(2,1)}, bf16[2,512,512]{1,2,0:T(8,128)(2,1)S(1)}, u32[]{:S(2)}, u32[]{:S(2)}) %collective-permute-start.1) | collective-permute-done | bytes 1048608 | tf_op jit(solution)/shard_map/while/body/eval_jaxpr/ppermute | solution.py:19
  771.8 28.7 %collective-permute-done.1 = bf16[2,512,512]{1,2,0:T(8,128)(2,1)S(1)} collective-permute-done((bf16[2,512,512]{1,2,0:T(8,128)(2,1)}, bf16[2,512,512]{1,2,0:T(8,128)(2,1)S(1)}, u32[]{:S(2)}, u32[]{:S(2)}) %collective-permute-start.1) | collective-permute-done | bytes 1048608 | tf_op jit(solution)/shard_map/while/body/eval_jaxpr/ppermute | solution.py:19
  821.3 21.8 %collective-permute-done.3 = bf16[2,512,512]{2,1,0:T(8,128)(2,1)S(1)} collective-permute-done((bf16[2,512,512]{2,1,0:T(8,128)(2,1)S(1)}, bf16[2,512,512]{2,1,0:T(8,128)(2,1)S(1)}, u32[]{:S(2)}, u32[]{:S(2)}) %collective-permute-start.3) | collective-permute-done | bytes 1048608 | tf_op jit(solution)/shard_map/ppermute | solution.py:19
  870.5 21.4 %reduce-scatter.5.cloned.1.call-done = bf16[512,3,512]{2,0,1:T(8,128)(2,1)} async-done(((bf16[1024,3,512]{2,0,1:T(8,128)(2,1)}), bf16[512,3,512]{2,0,1:T(8,128)(2,1)}) %reduce-scatter.5.cloned.1.call-update) | async-done | bytes 1572880 | tf_op jit(solution)/shard_map/reduce_scatter | solution.py:267
  891.9 70.0 %reduce-scatter.9.cloned.1.call-done = bf16[512,2,1312]{0,2,1:T(8,128)(2,1)} async-done(((bf16[1024,2,1312]{0,2,1:T(8,128)(2,1)}), bf16[512,2,1312]{0,2,1:T(8,128)(2,1)}) %reduce-scatter.9.cloned.1.call-update) | async-done | bytes 2686992 | tf_op jit(solution)/shard_map/reduce_scatter | solution.py:276
  963.8 22.4 %all-reduce.19.cloned.1.call-done = (bf16[512,1024]{1,0:T(8,128)(2,1)}, bf16[512,1024]{1,0:T(8,128)(2,1)}) async-done(((bf16[512,1024]{1,0:T(8,128)(2,1)}, bf16[512,1024]{1,0:T(8,128)(2,1)}), (bf16[512,1024]{1,0:T(8,128)(2,1)}, bf16[512,1024]{1,0:T(8,128)(2,1)})) %all-reduce.19.cloned.1.call-update) | async-done | bytes 2097168 | tf_op jit(solution)/shard_map/psum | solution.py:191
  994.3 22.4 %all-reduce.4 = (bf16[512]{0:T(512)(128)(2,1)S(1)}, bf16[512]{0:T(512)(128)(2,1)S(1)}) all-reduce(bf16[512]{0:T(512)(128)(2,1)S(1)} %dynamic-slice.1, bf16[512]{0:T(512)(128)(2,1)S(1)} %dynamic-slice.3), channel_id=1, replica_groups=mesh['shard'=2,'ctx'=8,'tp'=2] {'ctx'}, use_global_device_ids=true, to_apply=%region_29.30 | all-reduce | flops 1024 | bytes 4096 | tf_op jit(solution)/shard_map/psum | solution.py:284
  1021.7 182.1 %all-reduce.17.cloned.1.call-done = (bf16[512,3,512]{2,0,1:T(8,128)(2,1)}, bf16[512,512]{1,0:T(8,128)(2,1)}, bf16[512,2,1312]{0,2,1:T(8,128)(2,1)}, bf16[1312,512]{1,0:T(8,128)(2,1)}) async-done(((bf16[512,3,512]{2,0,1:T(8,128)(2,1)}, bf16[512,512]{1,0:T(8,128)(2,1)}, bf16[512,2,1312]{0,2,1:T(8,128)(2,1)}, bf16[1312,512]{1,0:T(8,128)(2,1)}), (bf16[512,3,512]{2,0,1:T(8,128)(2,1)}, ...) | async-done | bytes 6127632 | tf_op jit(solution)/shard_map/psum | solution.py:285
  (480 shorter events, 387.0 us)
Async XLA Ops:
  7.2 50.6 %all-gather.7.cloned.1.call-start = ((), (), s32[]{:S(2)}) async-start(), calls=%async_computation.4 | async-start | bytes 4718592 | tf_op jit(solution)/shard_map/all_gather | solution.py:136
  9.9 291.7 %all-gather.9.cloned.1.call-start = ((), (), s32[]{:S(2)}) async-start(), calls=%async_computation.5 | async-start | bytes 1572864 | tf_op jit(solution)/shard_map/all_gather | solution.py:137
  10.7 299.2 %all-gather.13.cloned.1.call-start = ((), (), s32[]{:S(2)}) async-start(), calls=%async_computation.8 | async-start | bytes 4030464 | tf_op jit(solution)/shard_map/all_gather | solution.py:183
  11.4 310.2 %all-reduce.13.cloned.1.call-start = ((), (), s32[]{:S(2)}) async-start(), calls=%async_computation.6 | async-start | bytes 2097152 | tf_op jit(solution)/shard_map/psum | solution.py:179
  304.8 89.5 %all-gather.11.cloned.1.call-start = ((), (), s32[]{:S(2)}) async-start(), calls=%async_computation.7 | async-start | bytes 8060928 | tf_op jit(solution)/shard_map/all_gather | solution.py:182
  305.4 128.4 %all-reduce.15.cloned.1.call-start = ((), (), s32[]{:S(2)}) async-start(), calls=%async_computation.9 | async-start | bytes 2097152 | tf_op jit(solution)/shard_map/psum | solution.py:202
  414.1 456.4 %reduce-scatter.7.cloned.1.call-start = ((), (), s32[]{:S(2)}) async-start(), calls=%async_computation.11 | async-start | bytes 1572864 | tf_op jit(solution)/shard_map/reduce_scatter | solution.py:270
  441.5 429.1 %reduce-scatter.11.cloned.1.call-start = ((), (), s32[]{:S(2)}) async-start(), calls=%async_computation.13 | async-start | bytes 4030464 | tf_op jit(solution)/shard_map/reduce_scatter | solution.py:279
  446.0 445.9 %reduce-scatter.5.cloned.1.call-start = ((), (), s32[]{:S(2)}) async-start(), calls=%async_computation.10 | async-start | bytes 4718592 | tf_op jit(solution)/shard_map/reduce_scatter | solution.py:267
  465.8 49.2 %collective-permute-start.2 = (bf16[2,512,512]{1,2,0:T(8,128)(2,1)}, bf16[2,512,512]{1,2,0:T(8,128)(2,1)}, u32[]{:S(2)}, u32[]{:S(2)}) collective-permute-start(bf16[2,512,512]{1,2,0:T(8,128)(2,1)} %get-tuple-element.885), channel_id=1, source_target_pairs={{14,0},{0,2},{2,4},{4,6},{6,8},{8,10},{10,12},{12,14},{15,1},{1,3}... | collective-permute-start | bytes 3145736 | tf_op jit(solution)/shard_map/while/body/eval_jaxpr/ppermute | solution.py:19
  517.5 50.1 %collective-permute-start.2 = (bf16[2,512,512]{1,2,0:T(8,128)(2,1)}, bf16[2,512,512]{1,2,0:T(8,128)(2,1)}, u32[]{:S(2)}, u32[]{:S(2)}) collective-permute-start(bf16[2,512,512]{1,2,0:T(8,128)(2,1)} %get-tuple-element.885), channel_id=1, source_target_pairs={{14,0},{0,2},{2,4},{4,6},{6,8},{8,10},{10,12},{12,14},{15,1},{1,3}... | collective-permute-start | bytes 3145736 | tf_op jit(solution)/shard_map/while/body/eval_jaxpr/ppermute | solution.py:19
  570.1 29.0 %collective-permute-start.1 = (bf16[2,512,512]{1,2,0:T(8,128)(2,1)}, bf16[2,512,512]{1,2,0:T(8,128)(2,1)S(1)}, u32[]{:S(2)}, u32[]{:S(2)}) collective-permute-start(bf16[2,512,512]{1,2,0:T(8,128)(2,1)} %get-tuple-element.884), channel_id=1, source_target_pairs={{14,0},{0,2},{2,4},{4,6},{6,8},{8,10},{10,12},{12,14},{15,1},{1,3}... | collective-permute-start | bytes 3145736 | tf_op jit(solution)/shard_map/while/body/eval_jaxpr/ppermute | solution.py:19
  570.1 49.2 %collective-permute-start.2 = (bf16[2,512,512]{1,2,0:T(8,128)(2,1)}, bf16[2,512,512]{1,2,0:T(8,128)(2,1)}, u32[]{:S(2)}, u32[]{:S(2)}) collective-permute-start(bf16[2,512,512]{1,2,0:T(8,128)(2,1)} %get-tuple-element.885), channel_id=1, source_target_pairs={{14,0},{0,2},{2,4},{4,6},{6,8},{8,10},{10,12},{12,14},{15,1},{1,3}... | collective-permute-start | bytes 3145736 | tf_op jit(solution)/shard_map/while/body/eval_jaxpr/ppermute | solution.py:19
  621.8 29.0 %collective-permute-start.1 = (bf16[2,512,512]{1,2,0:T(8,128)(2,1)}, bf16[2,512,512]{1,2,0:T(8,128)(2,1)S(1)}, u32[]{:S(2)}, u32[]{:S(2)}) collective-permute-start(bf16[2,512,512]{1,2,0:T(8,128)(2,1)} %get-tuple-element.884), channel_id=1, source_target_pairs={{14,0},{0,2},{2,4},{4,6},{6,8},{8,10},{10,12},{12,14},{15,1},{1,3}... | collective-permute-start | bytes 3145736 | tf_op jit(solution)/shard_map/while/body/eval_jaxpr/ppermute | solution.py:19
  621.8 48.3 %collective-permute-start.2 = (bf16[2,512,512]{1,2,0:T(8,128)(2,1)}, bf16[2,512,512]{1,2,0:T(8,128)(2,1)}, u32[]{:S(2)}, u32[]{:S(2)}) collective-permute-start(bf16[2,512,512]{1,2,0:T(8,128)(2,1)} %get-tuple-element.885), channel_id=1, source_target_pairs={{14,0},{0,2},{2,4},{4,6},{6,8},{8,10},{10,12},{12,14},{15,1},{1,3}... | collective-permute-start | bytes 3145736 | tf_op jit(solution)/shard_map/while/body/eval_jaxpr/ppermute | solution.py:19
  672.7 29.0 %collective-permute-start.1 = (bf16[2,512,512]{1,2,0:T(8,128)(2,1)}, bf16[2,512,512]{1,2,0:T(8,128)(2,1)S(1)}, u32[]{:S(2)}, u32[]{:S(2)}) collective-permute-start(bf16[2,512,512]{1,2,0:T(8,128)(2,1)} %get-tuple-element.884), channel_id=1, source_target_pairs={{14,0},{0,2},{2,4},{4,6},{6,8},{8,10},{10,12},{12,14},{15,1},{1,3}... | collective-permute-start | bytes 3145736 | tf_op jit(solution)/shard_map/while/body/eval_jaxpr/ppermute | solution.py:19
  672.7 47.3 %collective-permute-start.2 = (bf16[2,512,512]{1,2,0:T(8,128)(2,1)}, bf16[2,512,512]{1,2,0:T(8,128)(2,1)}, u32[]{:S(2)}, u32[]{:S(2)}) collective-permute-start(bf16[2,512,512]{1,2,0:T(8,128)(2,1)} %get-tuple-element.885), channel_id=1, source_target_pairs={{14,0},{0,2},{2,4},{4,6},{6,8},{8,10},{10,12},{12,14},{15,1},{1,3}... | collective-permute-start | bytes 3145736 | tf_op jit(solution)/shard_map/while/body/eval_jaxpr/ppermute | solution.py:19
  722.5 29.0 %collective-permute-start.1 = (bf16[2,512,512]{1,2,0:T(8,128)(2,1)}, bf16[2,512,512]{1,2,0:T(8,128)(2,1)S(1)}, u32[]{:S(2)}, u32[]{:S(2)}) collective-permute-start(bf16[2,512,512]{1,2,0:T(8,128)(2,1)} %get-tuple-element.884), channel_id=1, source_target_pairs={{14,0},{0,2},{2,4},{4,6},{6,8},{8,10},{10,12},{12,14},{15,1},{1,3}... | collective-permute-start | bytes 3145736 | tf_op jit(solution)/shard_map/while/body/eval_jaxpr/ppermute | solution.py:19
  722.5 46.4 %collective-permute-start.2 = (bf16[2,512,512]{1,2,0:T(8,128)(2,1)}, bf16[2,512,512]{1,2,0:T(8,128)(2,1)}, u32[]{:S(2)}, u32[]{:S(2)}) collective-permute-start(bf16[2,512,512]{1,2,0:T(8,128)(2,1)} %get-tuple-element.885), channel_id=1, source_target_pairs={{14,0},{0,2},{2,4},{4,6},{6,8},{8,10},{10,12},{12,14},{15,1},{1,3}... | collective-permute-start | bytes 3145736 | tf_op jit(solution)/shard_map/while/body/eval_jaxpr/ppermute | solution.py:19
  771.5 29.0 %collective-permute-start.1 = (bf16[2,512,512]{1,2,0:T(8,128)(2,1)}, bf16[2,512,512]{1,2,0:T(8,128)(2,1)S(1)}, u32[]{:S(2)}, u32[]{:S(2)}) collective-permute-start(bf16[2,512,512]{1,2,0:T(8,128)(2,1)} %get-tuple-element.884), channel_id=1, source_target_pairs={{14,0},{0,2},{2,4},{4,6},{6,8},{8,10},{10,12},{12,14},{15,1},{1,3}... | collective-permute-start | bytes 3145736 | tf_op jit(solution)/shard_map/while/body/eval_jaxpr/ppermute | solution.py:19
  771.5 45.5 %collective-permute-start.2 = (bf16[2,512,512]{1,2,0:T(8,128)(2,1)}, bf16[2,512,512]{1,2,0:T(8,128)(2,1)}, u32[]{:S(2)}, u32[]{:S(2)}) collective-permute-start(bf16[2,512,512]{1,2,0:T(8,128)(2,1)} %get-tuple-element.885), channel_id=1, source_target_pairs={{14,0},{0,2},{2,4},{4,6},{6,8},{8,10},{10,12},{12,14},{15,1},{1,3}... | collective-permute-start | bytes 3145736 | tf_op jit(solution)/shard_map/while/body/eval_jaxpr/ppermute | solution.py:19
  851.5 110.4 %reduce-scatter.9.cloned.1.call-start = ((), (), s32[]{:S(2)}) async-start(), calls=%async_computation.12 | async-start | bytes 8060928 | tf_op jit(solution)/shard_map/reduce_scatter | solution.py:276
  861.6 124.6 %all-reduce.19.cloned.1.call-start = ((), (), s32[]{:S(2)}) async-start(), calls=%async_computation.15 | async-start | bytes 4194304 | tf_op jit(solution)/shard_map/psum | solution.py:191
  870.4 333.3 %all-reduce.17.cloned.1.call-start = ((), (), s32[]{:S(2)}) async-start(), calls=%async_computation.14 | async-start | bytes 12255232 | tf_op jit(solution)/shard_map/psum | solution.py:285
  (99 other events, 817.4 us)
Sparse Core Ops, SparseCore 0:
  10.1 47.6 all-gather.6
  59.4 21.3 all-gather.8
  82.3 39.7 all-gather.12
  304.9 16.6 all-reduce.12
  323.1 71.2 all-gather.10
  414.2 19.5 all-reduce.14
  441.6 21.4 reduce-scatter.6
  465.5 38.2 reduce-scatter.10
  851.6 40.2 reduce-scatter.4
  894.7 67.1 reduce-scatter.8
  964.9 21.2 all-reduce.18
  991.4 212.2 all-reduce.16
where the time goes:
time: 1230 us; the launch traced here: 1220 us
  waiting for transfers between devices  882 us (72%)
  matrix products  163 us (13%)
  other arithmetic  79 us (6%)
  blocking collectives  36.9 us (3%)
  local copies, waits for them, and re-layouts  35.1 us (3%)
  between operations  15.8 us (1%)
    ppermute x22, waiting for transfers between devices, shifted(): return lax.ppermute(block, axis, route)  449 us
    psum x1, waiting for transfers between devices, shards(): lax.psum(sharded[1].astype(jnp.bfloat16), 'ctx').astype(jnp.float32)  182 us
    all_gather x1, waiting for transfers between devices, shards(): lax.all_gather(w_in, 'shard', axis=0, tiled=True)  70.5 us
    reduce_scatter x1, waiting for transfers between devices, shards(): lax.psum_scatter(grad_in.astype(jnp.bfloat16), 'shard', scatter_dimension...  70 us
    all_gather x1, waiting for transfers between devices, shards(): lax.all_gather(w_qkv, 'shard', axis=0, tiled=True)  38.1 us
    dot_general x8, matrix products, backward_step(): jnp.einsum('qhd,khd->hqk', grad_heads, values, preferred_element_type=jnp...  30.7 us
  transfers between devices with their start and end apart: 34, of which 30 were waited for; matrix products, arithmetic and copies ran while one was open for 19% of the time, Pallas kernels for 0%

commit v1 on v0

--- a/solution.py
+++ b/solution.py
@@ -1,8 +1,11 @@
+import functools
 import math
 
 import jax
 import jax.numpy as jnp
 from jax import lax
+from jax.experimental import pallas as pl
+from jax.experimental.pallas import tpu as pltpu
 from jax.sharding import PartitionSpec as P
 
 HD = 64
@@ -291,9 +294,321 @@
     return (output, grad_tokens, summed[0], summed[1], summed[2], summed[3], summed[4], summed[5])
 
 
+LOG2E = 1.4426950408889634
+VMEM_BYTES = 56 * 1024 * 1024
+
+
+def rope_tables_t(places, head_size):
+    half_size = head_size // 2
+    powers = jnp.arange(half_size, dtype=jnp.float32) * (-2.0 * math.log(ROPE_BASE) / head_size)
+    angles = jnp.exp(powers)[:, None] * places.astype(jnp.float32)[None, :]
+    return (jnp.cos(angles), jnp.sin(angles))
+
+
+def rotate_t(values, cos_t, sin_t):
+    half_size = values.shape[-2] // 2
+    front, back = values[..., :half_size, :], values[..., half_size:, :]
+    return jnp.concatenate(
+        [front * cos_t - back * sin_t, back * cos_t + front * sin_t], axis=-2
+    )
+
+
+def segment_ids(ends_ref, positions):
+    ids = jnp.zeros(positions.shape, jnp.int32)
+    for i in range(ends_ref.shape[1]):
+        ids += (positions >= ends_ref[0, i]).astype(jnp.int32)
+    return ids
+
+
+def forward_kernel(blocks, ends_ref, q_ref, k_ref, v_ref, low_ref, out_ref, lse_ref, v_rows):
+    step = pl.program_id(1)
+    size = q_ref.shape[3]
+
+    @pl.when(step == 0)
+    def _():
+        lane = lax.broadcasted_iota(jnp.int32, (size, HD), 1)
+        ones = jnp.where(lane == 0, 1.0, 0.0).astype(jnp.bfloat16)
+        for j in range(blocks):
+            v_rows[j, :, :HD] = v_ref[j, 0].T
+            v_rows[j, :, HD:] = ones
+
+    queries = q_ref[0, 0].T
+    scale = LOG2E / math.sqrt(HD)
+
+    def run(masked):
+        rows_id = None
+        scores = []
+        top = None
+        for j in range(blocks):
+            part = jnp.dot(queries, k_ref[j, 0], preferred_element_type=jnp.float32)
+            if masked or j in (0, blocks - 1):
+                if rows_id is None:
+                    rows_id = segment_ids(
+                        ends_ref, step * size + lax.broadcasted_iota(jnp.int32, (size, 1), 0)
+                    )
+                keys_id = segment_ids(
+                    ends_ref, j * size + lax.broadcasted_iota(jnp.int32, (1, size), 1)
+                )
+                part = jnp.where(rows_id == keys_id, part, MASKED)
+            scores.append(part)
+            most = jnp.max(part, axis=1, keepdims=True)
+            top = most if top is None else jnp.maximum(top, most)
+        offset = top * scale
+        total = None
+        for j in range(blocks):
+            raised = jnp.exp2(scores[j] * scale - offset).astype(jnp.bfloat16)
+            part = jnp.dot(raised, v_rows[j], preferred_element_type=jnp.float32)
+            total = part if total is None else total + part
+        flat = total.T
+        sums = flat[HD : HD + 1]
+        result = flat[:HD] / sums
+        out_ref[0, 0] = result
+        low_ref[0, 0] = result.astype(jnp.bfloat16)
+        lse_ref[0, 0] = offset.T + jnp.log2(sums)
+
+    edge = (step == 0) | (step == blocks - 1)
+    pl.when(edge)(lambda: run(True))
+    pl.when(jnp.logical_not(edge))(lambda: run(False))
+
+
+def backward_kernel(
+    blocks, ends_ref, q_ref, k_ref, v_ref, do_ref, o_ref, lse_ref, grad_ref, k_rows, v_rows, dk, dv
+):
+    step = pl.program_id(1)
+    size = q_ref.shape[3]
+
+    @pl.when(step == 0)
+    def _():
+        for j in range(blocks):
+            k_rows[j] = k_ref[j, 0].T
+            v_rows[j] = v_ref[j, 0].T
+        dk[...] = jnp.zeros_like(dk)
+        dv[...] = jnp.zeros_like(dv)
+
+    scale = LOG2E / math.sqrt(HD)
+    queries_t = q_ref[0, 0]
+    queries = queries_t.T
+    grads_t = do_ref[0, 0]
+    grads = grads_t.T
+    delta = jnp.sum(grads_t.astype(jnp.float32) * o_ref[0, 0], axis=0, keepdims=True)
+    lse = lse_ref[0, 0]
+
+    def run(masked):
+        dq = jnp.zeros((size, HD), jnp.float32)
+        queries_id = None
+        for j in range(blocks):
+            scores = jnp.dot(k_rows[j], queries_t, preferred_element_type=jnp.float32)
+            weights = jnp.exp2(scores * scale - lse)
+            if masked or j in (0, blocks - 1):
+                if queries_id is None:
+                    queries_id = segment_ids(
+                        ends_ref, step * size + lax.broadcasted_iota(jnp.int32, (1, size), 1)
+                    )
+                keys_id = segment_ids(
+                    ends_ref, j * size + lax.broadcasted_iota(jnp.int32, (size, 1), 0)
+                )
+                weights = jnp.where(queries_id == keys_id, weights, 0.0)
+            grad_weights = jnp.dot(v_rows[j], grads_t, preferred_element_type=jnp.float32)
+            grad_scores = (weights * (grad_weights - delta)).astype(jnp.bfloat16)
+            dv[j] += jnp.dot(
+                weights.astype(jnp.bfloat16), grads, preferred_element_type=jnp.float32
+            )
+            dk[j] += jnp.dot(grad_scores, queries, preferred_element_type=jnp.float32)
+            dq += lax.dot_general(
+                grad_scores, k_rows[j], (((0,), (0,)), ((), ())), preferred_element_type=jnp.float32
+            )
+        grad_ref[step, 0, :HD] = (dq * (1.0 / math.sqrt(HD))).T.astype(jnp.bfloat16)
+
+    edge = (step == 0) | (step == blocks - 1)
+    pl.when(edge)(lambda: run(True))
+    pl.when(jnp.logical_not(edge))(lambda: run(False))
+
+    @pl.when(step == blocks - 1)
+    def _():
+        for j in range(blocks):
+            grad_ref[j, 0, HD : 2 * HD] = (dk[j] * (1.0 / math.sqrt(HD))).T.astype(jnp.bfloat16)
+            grad_ref[j, 0, 2 * HD :] = dv[j].T.astype(jnp.bfloat16)
+
+
+def packed_specs(blocks, size):
+    return [
+        pl.BlockSpec(memory_space=pltpu.SMEM),
+        pl.BlockSpec((1, 1, HD, size), lambda h, i: (i, h, 0, 0)),
+        pl.BlockSpec((blocks, 1, HD, size), lambda h, i: (0, h, 1, 0)),
+        pl.BlockSpec((blocks, 1, HD, size), lambda h, i: (0, h, 2, 0)),
+    ]
+
+
+def attention_forward(ends, packed):
+    blocks, heads, _, size = packed.shape
+    pairs = heads * (blocks * size) ** 2
+    tile = pl.BlockSpec((1, 1, HD, size), lambda h, i: (i, h, 0, 0))
+    line = pl.BlockSpec((1, 1, 1, size), lambda h, i: (i, h, 0, 0))
+    return pl.pallas_call(
+        functools.partial(forward_kernel, blocks),
+        grid=(heads, blocks),
+        in_specs=packed_specs(blocks, size),
+        out_specs=[tile, tile, line],
+        out_shape=[
+            jax.ShapeDtypeStruct((blocks, heads, HD, size), jnp.bfloat16),
+            jax.ShapeDtypeStruct((blocks, heads, HD, size), jnp.float32),
+            jax.ShapeDtypeStruct((blocks, heads, 1, size), jnp.float32),
+        ],
+        scratch_shapes=[pltpu.VMEM((blocks, size, 2 * HD), jnp.bfloat16)],
+        compiler_params=pltpu.CompilerParams(vmem_limit_bytes=VMEM_BYTES),
+        cost_estimate=pl.CostEstimate(
+            flops=16 * HD * pairs, bytes_accessed=packed.size * 6, transcendentals=pairs
+        ),
+        name="attention_forward",
+    )(ends, packed, packed, packed)
+
+
+def attention_backward(ends, packed, grads, attended, lse):
+    blocks, heads, _, size = packed.shape
+    pairs = heads * (blocks * size) ** 2
+    tile = pl.BlockSpec((1, 1, HD, size), lambda h, i: (i, h, 0, 0))
+    line = pl.BlockSpec((1, 1, 1, size), lambda h, i: (i, h, 0, 0))
+    return pl.pallas_call(
+        functools.partial(backward_kernel, blocks),
+        grid=(heads, blocks),
+        in_specs=packed_specs(blocks, size) + [tile, tile, line],
+        out_specs=pl.BlockSpec((blocks, 1, 3 * HD, size), lambda h, i: (0, h, 0, 0)),
+        out_shape=jax.ShapeDtypeStruct(packed.shape, jnp.bfloat16),
+        scratch_shapes=[
+            pltpu.VMEM((blocks, size, HD), jnp.bfloat16),
+            pltpu.VMEM((blocks, size, HD), jnp.bfloat16),
+            pltpu.VMEM((blocks, size, HD), jnp.float32),
+            pltpu.VMEM((blocks, size, HD), jnp.float32),
+        ],
+        compiler_params=pltpu.CompilerParams(vmem_limit_bytes=VMEM_BYTES),
+        cost_estimate=pl.CostEstimate(
+            flops=40 * HD * pairs, bytes_accessed=packed.size * 10, transcendentals=pairs
+        ),
+        name="attention_backward",
+    )(ends, packed, packed, packed, grads, attended, lse)
+
+
+def exchanged(array_in):
+    return lax.all_to_all(array_in, "ctx", split_axis=0, concat_axis=0, tiled=True)
+
+
+def head_shards(tokens, cotangent, lengths, g_attn, w_qkv, w_attn_out, g_mlp, w_in, w_mlp_out):
+    tok_rows = tokens.shape[0]
+    ctx_size = lax.axis_size("ctx")
+    ctx_place = lax.axis_index("ctx")
+    row_index = jnp.arange(tok_rows, dtype=jnp.int32)
+    _, inside = positions_of(lengths[0], ctx_place * tok_rows + row_index)
+    cos_t, sin_t = rope_tables_t(inside, HD)
+    ends = jnp.cumsum(lengths, axis=1).astype(jnp.int32)
+
+    attn_gain, qkv_full = (
+        lax.all_gather(g_attn, "shard", axis=0, tiled=True),
+        lax.all_gather(w_qkv, "shard", axis=0, tiled=True),
+    )
+    out_full = lax.all_gather(w_attn_out, "shard", axis=1, tiled=True)
+    residual = tokens.astype(jnp.float32)
+    normed_one, norm_one_back = jax.vjp(layer_norm, residual, attn_gain.astype(jnp.float32))
+    hidden_one = normed_one.astype(jnp.bfloat16)
+    projected = jnp.einsum("td,dcn->cnt", hidden_one, qkv_full, preferred_element_type=jnp.float32)
+    local_width = projected.shape[1]
+    head_count = local_width // HD
+    own_heads = head_count // ctx_size
+    split_heads = projected.reshape(3, head_count, HD, tok_rows)
+    packed = jnp.concatenate(
+        [
+            rotate_t(split_heads[0], cos_t, sin_t).astype(jnp.bfloat16),
+            rotate_t(split_heads[1], cos_t, sin_t).astype(jnp.bfloat16),
+            split_heads[2].astype(jnp.bfloat16),
+        ],
+        axis=1,
+    ).reshape(ctx_size, own_heads, 3 * HD, tok_rows)
+    packed = exchanged(packed)
+    own_low, own_attended, lse = attention_forward(ends, packed)
+    attn_low = exchanged(own_low).reshape(local_width, tok_rows)
+    attn_part = jnp.einsum("nt,nd->td", attn_low, out_full, preferred_element_type=jnp.float32)
+    middle = residual + lax.psum(attn_part.astype(jnp.bfloat16), "tp").astype(jnp.float32)
+    mlp_gain, in_full, down_full = (
+        lax.all_gather(g_mlp, "shard", axis=0, tiled=True),
+        lax.all_gather(w_in, "shard", axis=0, tiled=True),
+        lax.all_gather(w_mlp_out, "shard", axis=1, tiled=True),
+    )
+    normed_two, norm_two_back = jax.vjp(layer_norm, middle, mlp_gain.astype(jnp.float32))
+    hidden_two = normed_two.astype(jnp.bfloat16)
+    lifted = jnp.einsum("td,dcf->tcf", hidden_two, in_full, preferred_element_type=jnp.float32)
+    mixed_f, geglu_back = jax.vjp(geglu, lifted)
+    mixed_low = mixed_f.astype(jnp.bfloat16)
+    mlp_part = jnp.dot(mixed_low, down_full, preferred_element_type=jnp.float32)
+    output = (middle + lax.psum(mlp_part.astype(jnp.bfloat16), "tp").astype(jnp.float32)).astype(
+        jnp.bfloat16
+    )
+    grad_down = jnp.einsum("tf,td->fd", mixed_low, cotangent, preferred_element_type=jnp.float32)
+    grad_mixed = jnp.einsum("td,fd->tf", cotangent, down_full, preferred_element_type=jnp.float32)
+    (grad_lifted,) = geglu_back(grad_mixed)
+    lifted_low = grad_lifted.astype(jnp.bfloat16)
+    grad_in = jnp.einsum("td,tcf->dcf", hidden_two, lifted_low, preferred_element_type=jnp.float32)
+    hidden_two_part = jnp.einsum(
+        "tcf,dcf->td", lifted_low, in_full, preferred_element_type=jnp.float32
+    )
+    grad_hidden_two = lax.psum(hidden_two_part.astype(jnp.bfloat16), "tp").astype(jnp.float32)
+    grad_middle_norm, grad_mlp_gain = norm_two_back(grad_hidden_two)
+    grad_middle = cotangent.astype(jnp.float32) + grad_middle_norm
+    grad_branch = grad_middle.astype(jnp.bfloat16)
+    grad_attn_out = jnp.einsum(
+        "nt,td->nd", attn_low, grad_branch, preferred_element_type=jnp.float32
+    )
+    grad_attended = jnp.einsum(
+        "td,nd->nt", grad_branch, out_full, preferred_element_type=jnp.float32
+    ).astype(jnp.bfloat16)
+    own_grads = exchanged(grad_attended.reshape(ctx_size, own_heads, HD, tok_rows))
+    own_packed = attention_backward(ends, packed, own_grads, own_attended, lse)
+    grad_packed = exchanged(own_packed).reshape(head_count, 3, HD, tok_rows)
+    grad_projected = jnp.stack(
+        [
+            rotate_t(grad_packed[:, 0].astype(jnp.float32), cos_t, -sin_t).astype(jnp.bfloat16),
+            rotate_t(grad_packed[:, 1].astype(jnp.float32), cos_t, -sin_t).astype(jnp.bfloat16),
+            grad_packed[:, 2],
+        ],
+        axis=0,
+    ).reshape(3, local_width, tok_rows)
+    grad_qkv = jnp.einsum(
+        "td,cnt->dcn", hidden_one, grad_projected, preferred_element_type=jnp.float32
+    )
+    hidden_one_part = jnp.einsum(
+        "cnt,dcn->td", grad_projected, qkv_full, preferred_element_type=jnp.float32
+    )
+    grad_hidden_one = lax.psum(hidden_one_part.astype(jnp.bfloat16), "tp").astype(jnp.float32)
+    grad_input_norm, grad_attn_gain = norm_one_back(grad_hidden_one)
+    grad_tokens = (grad_middle + grad_input_norm).astype(jnp.bfloat16)
+
+    def owned(partial, dimension):
+        part = lax.psum_scatter(
+            partial.astype(jnp.bfloat16), "shard", scatter_dimension=dimension, tiled=True
+        )
+        return lax.psum(part, "ctx").astype(jnp.float32)
+
+    return (
+        output,
+        grad_tokens,
+        owned(grad_attn_gain, 0),
+        owned(grad_qkv, 0),
+        owned(grad_attn_out, 1),
+        owned(grad_mlp_gain, 0),
+        owned(grad_in, 0),
+        owned(grad_down, 1),
+    )
+
+
+def layer(tokens, cotangent, lengths, g_attn, w_qkv, w_attn_out, g_mlp, w_in, w_mlp_out):
+    head_count = w_qkv.shape[2] // HD
+    whole_heads = head_count % lax.axis_size("ctx") == 0
+    return (head_shards if whole_heads else shards)(
+        tokens, cotangent, lengths, g_attn, w_qkv, w_attn_out, g_mlp, w_in, w_mlp_out
+    )
+
+
 def solution(mesh):
     return jax.shard_map(
-        shards,
+        layer,
         mesh=mesh,
         in_specs=(
             P(("shard", "ctx"), None),

time: 1230 us -> 762 us (0.62)
  waiting for transfers between devices: 882 us -> 428 us
  matrix products: 163 us -> 50.1 us
  Pallas kernels: 0 us -> 98.1 us
  blocking collectives: 36.9 us -> 98.4 us
  other arithmetic: 79 us -> 40.5 us
  local copies, waits for them, and re-layouts: 35.1 us -> 16.7 us
    ppermute x22 -> x0, waiting for transfers between devices: 449 us -> none  [shifted(): return lax.ppermute(block, axis, route)]
    dot_general x67 -> x12, matrix products: 163 us -> 50.1 us  [the longest x1 8.05 us: head_shards(): jnp.einsum('td,tcf->dcf', hidden_two, lifted_low, preferred_element_type=...]
    pallas_call x0 -> x2, Pallas kernels: none -> 98.1 us  [the longest x1 51.6 us: attention_backward(): pl.pallas_call(functools.partial(backward_kernel, blocks), grid=(heads, b...]
    all_to_all x0 -> x2, blocking collectives: none -> 61.2 us  [exchanged(): lax.all_to_all(array_in, 'ctx', split_axis=0, concat_axis=0, tiled=True)]
    reduce_scatter x4, waiting for transfers between devices: 91.4 us -> 33.7 us  [owned(): lax.psum_scatter(partial.astype(jnp.bfloat16), 'shard', scatter_dimension...]
    all_to_all x0 -> x2, waiting for transfers between devices: none -> 49.5 us  [exchanged(): lax.all_to_all(array_in, 'ctx', split_axis=0, concat_axis=0, tiled=True)]
    add x30 -> x1, other arithmetic: 17.9 us -> 0.01 us  [head_shards(): _, inside = positions_of(lengths[0], ctx_place * tok_rows + row_index)]
    while x92 -> x0, local copies, waits for them, and re-layouts: 17.9 us -> none
  transfers between devices with their start and end apart: 34 -> 14, of which waited for: 30 -> 9; matrix products, arithmetic and copies ran while one was open for 19% -> 7% of each run, Pallas kernels for 0% -> 13%
where the time goes in v1:
time: 762 us; the launch traced here: 758 us
  waiting for transfers between devices  428 us (56%)
  blocking collectives  98.4 us (13%)
  Pallas kernels  98.1 us (13%)
  matrix products  50.1 us (7%)
  other arithmetic  40.5 us (5%)
  local copies, waits for them, and re-layouts  16.7 us (2%)
  between operations  15.4 us (2%)
  starting transfers between devices  10.3 us (1%)
    psum x1, waiting for transfers between devices, owned(): return lax.psum(part, 'ctx').astype(jnp.float32)  182 us
    all_gather x1, waiting for transfers between devices, head_shards(): lax.all_gather(w_in, 'shard', axis=0, tiled=True)  70.5 us
    all_to_all x2, blocking collectives, exchanged(): lax.all_to_all(array_in, 'ctx', split_axis=0, concat_axis=0, tiled=True)  61.2 us
    pallas_call x1, Pallas kernels, attention_backward(): pl.pallas_call(functools.partial(backward_kernel, blocks), grid=(heads, b...  51.6 us
    all_to_all x2, waiting for transfers between devices, exchanged(): lax.all_to_all(array_in, 'ctx', split_axis=0, concat_axis=0, tiled=True)  49.5 us
    pallas_call x1, Pallas kernels, attention_forward(): pl.pallas_call(functools.partial(forward_kernel, blocks), grid=(heads, bl...  46.5 us
    all_gather x1, waiting for transfers between devices, head_shards(): lax.all_gather(w_qkv, 'shard', axis=0, tiled=True)  41.2 us
    reduce_scatter x4, waiting for transfers between devices, owned(): lax.psum_scatter(partial.astype(jnp.bfloat16), 'shard', scatter_dimension...  33.7 us
  transfers between devices with their start and end apart: 14, of which 9 were waited for; matrix products, arithmetic and copies ran while one was open for 7% of the time, Pallas kernels for 13%

profile of v1, /device:TPU:0, one launch (start us, length us, event | category | flops | bytes accessed | tf_op | source)
XLA Modules:
  0.0 757.8 jit_solution(645697211911416476)
XLA Ops:
  10.0 5.3 all-gather
  16.6 41.2 %all-gather.7.cloned.1.call-done = bf16[1024,3,512]{0,2,1:T(8,128)(2,1)} async-done(((bf16[512,3,512]{0,2,1:T(8,128)(2,1)}), bf16[1024,3,512]{0,2,1:T(8,128)(2,1)}) %all-gather.7.cloned.1.call-update) | async-done | bytes 3145744 | tf_op jit(solution)/shard_map/all_gather | solution.py:506
  66.2 5.5 all-to-all-start
  73.9 34.8 %all-to-all-done.q_ref.k_ref.v_ref = bf16[8,1,192,512]{3,2,1,0:T(8,128)(2,1)S(1)} async-done(((bf16[8,1,192,512]{3,2,1,0:T(8,128)(2,1)}), bf16[8,1,192,512]{3,2,1,0:T(8,128)(2,1)S(1)}, u32[]{:S(2)}, u32[]{:S(2)}) %all-to-all-start) | async-done | bytes 1572896 | tf_op jit(solution)/shard_map/all_to_all | solution.py:492
  109.9 46.5 %attention_forward.1 = (bf16[8,1,64,512]{3,2,1,0:T(8,128)(2,1)}, f32[8,1,64,512]{3,2,1,0:T(8,128)}, f32[8,1,1,512]{3,2,1,0:T(1,128)}) custom-call(s32[1,4]{1,0:T(1,128)} %reduce_window_sum.18.ends_ref, bf16[8,1,192,512]{3,2,1,0:T(8,128)(2,1)} %copy-done.10, bf16[8,1,192,512]{3,2,1,0:T(8,128)(2,1)} %copy-done.10, bf16[8,1,192,512]{3,2,1,0:T(8,128)(2,1)} %copy-done.10), custom_call_target="tpu_custom_call" | custom-call | flops 17179869184 | bytes 4718592 | tf_op jit(solution)/shard_map/attention_forward/pallas_call | solution.py:447
  160.1 14.6 %all-to-all-done.1 = bf16[8,1,64,512]{3,2,1,0:T(8,128)(2,1)S(1)} async-done(((bf16[8,1,64,512]{3,2,1,0:T(8,128)(2,1)}), bf16[8,1,64,512]{3,2,1,0:T(8,128)(2,1)S(1)}, u32[]{:S(2)}, u32[]{:S(2)}) %all-to-all-start.1) | async-done | bytes 524320 | tf_op jit(solution)/shard_map/all_to_all | solution.py:492
  178.6 4.6 all-gather.1
  183.2 5.0 fusion.66
  188.2 7.6 %all-reduce.13.cloned.1.call-done = bf16[512,1024]{1,0:T(8,128)(2,1)} async-done(((bf16[512,1024]{1,0:T(8,128)(2,1)}), bf16[512,1024]{1,0:T(8,128)(2,1)}) %all-reduce.13.cloned.1.call-update) | async-done | bytes 1048592 | tf_op jit(solution)/shard_map/psum | solution.py:529
  198.0 70.5 %all-gather.11.cloned.1.call-done = bf16[1024,2,1312]{0,2,1:T(8,128)(2,1)} async-done(((bf16[512,2,1312]{0,2,1:T(8,128)(2,1)}), bf16[1024,2,1312]{0,2,1:T(8,128)(2,1)}) %all-gather.11.cloned.1.call-update) | async-done | bytes 5373968 | tf_op jit(solution)/shard_map/all_gather | solution.py:532
  268.5 5.4 fusion.61
  274.0 5.8 multiply_bitcast_fusion
  288.5 19.3 %all-reduce.15.cloned.1.call-done = bf16[512,1024]{1,0:T(8,128)(2,1)} async-done(((bf16[512,1024]{1,0:T(8,128)(2,1)}), bf16[512,1024]{1,0:T(8,128)(2,1)}) %all-reduce.15.cloned.1.call-update) | async-done | bytes 1048592 | tf_op jit(solution)/shard_map/psum | solution.py:552
  320.2 8.1 %convolution_convert_fusion = bf16[1024,2,1312]{0,2,1:T(8,128)(2,1)} fusion(f32[512,1,1312]{0,2,1:T(8,128)} %copy-done.7, f32[512,1,1312]{0,2,1:T(8,128)} %copy-done.9, bf16[512,1024]{1,0:T(8,128)(2,1)S(1)} %copy-done.1, bf16[512,1024]{1,0:T(8,128)(2,1)S(1)} %copy-done, f32[1024]{0:T(1024)S(1)} %bitcast.181, f32[512]{0:T(512)S(1)} %fusion.54, ...), kind=kOutput, calls=%fused_computation.1 | convolution fusion | flops 2760507392 | bytes 12853248 | tf_op jit(solution)/shard_map/td,tcf->dcf/dot_general | solution.py:548
  331.4 20.6 %all_to_all.20.do_ref = bf16[8,1,64,512]{3,2,1,0:T(8,128)(2,1)} all-to-all(bf16[8,1,64,512]{3,2,1,0:T(8,128)(2,1)S(1)} %bitcast.172), channel_id=1, replica_groups=mesh['shard'=2,'ctx'=8,'tp'=2] {'ctx'}, dimensions={0} | all-to-all | bytes 1048576 | tf_op jit(solution)/shard_map/all_to_all | solution.py:492
  352.0 51.6 %attention_backward.1 = bf16[8,1,192,512]{3,2,1,0:T(8,128)(2,1)} custom-call(s32[1,4]{1,0:T(1,128)} %reduce_window_sum.18.ends_ref, bf16[8,1,192,512]{3,2,1,0:T(8,128)(2,1)} %copy-done.10, bf16[8,1,192,512]{3,2,1,0:T(8,128)(2,1)} %copy-done.10, bf16[8,1,192,512]{3,2,1,0:T(8,128)(2,1)} %copy-done.10, bf16[8,1,64,512]{3,2,1,0:T(8,128)(2,1)} %all_to_all.20.do_ref, ...), custom_call_target="tpu_custom_call" | custom-call | flops 42949672960 | bytes 7864320 | tf_op jit(solution)/shard_map/attention_backward/pallas_call | solution.py:471
  403.7 40.6 %all_to_all.21 = bf16[8,1,192,512]{3,2,1,0:T(8,128)(2,1)S(1)} all-to-all(bf16[8,1,192,512]{3,2,1,0:T(8,128)(2,1)} %attention_backward.1), channel_id=1, replica_groups=mesh['shard'=2,'ctx'=8,'tp'=2] {'ctx'}, dimensions={0} | all-to-all | bytes 3145728 | tf_op jit(solution)/shard_map/all_to_all | solution.py:492
  451.5 4.8 convolution_convert_fusion.2
  457.7 4.7 convolution_convert_fusion.3
  465.3 33.7 %reduce-scatter.5.cloned.1.call-done = bf16[512,3,512]{2,0,1:T(8,128)(2,1)} async-done(((bf16[1024,3,512]{2,0,1:T(8,128)(2,1)}), bf16[512,3,512]{2,0,1:T(8,128)(2,1)}) %reduce-scatter.5.cloned.1.call-update) | async-done | bytes 1572880 | tf_op jit(solution)/shard_map/reduce_scatter | solution.py:584
  500.9 22.4 %all-reduce.19.cloned.1.call-done = (bf16[512,1024]{1,0:T(8,128)(2,1)}, bf16[512,1024]{1,0:T(8,128)(2,1)}) async-done(((bf16[512,1024]{1,0:T(8,128)(2,1)}, bf16[512,1024]{1,0:T(8,128)(2,1)}), (bf16[512,1024]{1,0:T(8,128)(2,1)}, bf16[512,1024]{1,0:T(8,128)(2,1)})) %all-reduce.19.cloned.1.call-update) | async-done | bytes 2097168 | tf_op jit(solution)/shard_map/psum | solution.py:541
  526.3 4.9 all-reduce.7
  531.4 22.4 %all-reduce.4 = (bf16[512]{0:T(512)(128)(2,1)S(1)}, bf16[512]{0:T(512)(128)(2,1)S(1)}) all-reduce(bf16[512]{0:T(512)(128)(2,1)S(1)} %dynamic-slice.1, bf16[512]{0:T(512)(128)(2,1)S(1)} %dynamic-slice.3), channel_id=1, replica_groups=mesh['shard'=2,'ctx'=8,'tp'=2] {'ctx'}, use_global_device_ids=true, to_apply=%region_18.19 | all-reduce | flops 1024 | bytes 4096 | tf_op jit(solution)/shard_map/psum | solution.py:587
  558.7 182.1 %all-reduce.17.cloned.1.call-done = (bf16[512,3,512]{2,0,1:T(8,128)(2,1)}, bf16[512,512]{1,0:T(8,128)(2,1)}, bf16[512,2,1312]{0,2,1:T(8,128)(2,1)}, bf16[1312,512]{1,0:T(8,128)(2,1)}) async-done(((bf16[512,3,512]{2,0,1:T(8,128)(2,1)}, bf16[512,512]{1,0:T(8,128)(2,1)}, bf16[512,2,1312]{0,2,1:T(8,128)(2,1)}, bf16[1312,512]{1,0:T(8,128)(2,1)}), (bf16[512,3,512]{2,0,1:T(8,128)(2,1)}, ...) | async-done | bytes 6127632 | tf_op jit(solution)/shard_map/psum | solution.py:587
  (151 shorter events, 80.2 us)
Async XLA Ops:
  7.2 8.0 %copy-start.25 = (s32[1,4]{1,0:T(1,128)S(1)}, s32[1,4]{1,0:T(1,128)}, u32[]{:S(2)}) copy-start(s32[1,4]{1,0:T(1,128)} %param.11) | copy-start | bytes 52
  7.2 8.4 %copy-start = (bf16[512,1024]{1,0:T(8,128)(2,1)S(1)}, bf16[512,1024]{1,0:T(8,128)(2,1)}, u32[]{:S(2)}) copy-start(bf16[512,1024]{1,0:T(8,128)(2,1)} %param.9) | copy-start | bytes 3145732
  7.2 50.6 %all-gather.7.cloned.1.call-start = ((), (), s32[]{:S(2)}) async-start(), calls=%async_computation.8 | async-start | bytes 4718592 | tf_op jit(solution)/shard_map/all_gather | solution.py:506
  66.2 42.5 %all-to-all-start = ((bf16[8,1,192,512]{3,2,1,0:T(8,128)(2,1)}), bf16[8,1,192,512]{3,2,1,0:T(8,128)(2,1)S(1)}, u32[]{:S(2)}, u32[]{:S(2)}) async-start(bf16[8,1,192,512]{3,2,1,0:T(8,128)(2,1)} %bitcast.10), calls=%async_computation | async-start | bytes 3145728 | tf_op jit(solution)/shard_map/all_to_all | solution.py:492
  71.7 88.4 %all-gather.9.cloned.1.call-start = ((), (), s32[]{:S(2)}) async-start(), calls=%async_computation.9 | async-start | bytes 1572864 | tf_op jit(solution)/shard_map/all_gather | solution.py:508
  72.5 110.7 %all-gather.13.cloned.1.call-start = ((), (), s32[]{:S(2)}) async-start(), calls=%async_computation.12 | async-start | bytes 4030464 | tf_op jit(solution)/shard_map/all_gather | solution.py:533
  156.3 18.4 %all-to-all-start.1 = ((bf16[8,1,64,512]{3,2,1,0:T(8,128)(2,1)}), bf16[8,1,64,512]{3,2,1,0:T(8,128)(2,1)S(1)}, u32[]{:S(2)}, u32[]{:S(2)}) async-start(bf16[8,1,64,512]{3,2,1,0:T(8,128)(2,1)} %get-tuple-element.11), calls=%async_computation.1 | async-start | bytes 1048576 | tf_op jit(solution)/shard_map/all_to_all | solution.py:492
  160.1 35.7 %all-reduce.13.cloned.1.call-start = ((), (), s32[]{:S(2)}) async-start(), calls=%async_computation.10 | async-start | bytes 2097152 | tf_op jit(solution)/shard_map/psum | solution.py:529
  174.8 8.4 %copy-start.6 = (bf16[512,1024]{1,0:T(8,128)(2,1)S(1)}, bf16[512,1024]{1,0:T(8,128)(2,1)}, u32[]{:S(2)}) copy-start(bf16[512,1024]{1,0:T(8,128)(2,1)} %param.10) | copy-start | bytes 3145732
  177.9 90.6 %all-gather.11.cloned.1.call-start = ((), (), s32[]{:S(2)}) async-start(), calls=%async_computation.11 | async-start | bytes 8060928 | tf_op jit(solution)/shard_map/all_gather | solution.py:532
  178.5 129.3 %all-reduce.15.cloned.1.call-start = ((), (), s32[]{:S(2)}) async-start(), calls=%async_computation.13 | async-start | bytes 2097152 | tf_op jit(solution)/shard_map/psum | solution.py:552
  268.5 5.4 copy-start.3
  274.0 9.9 %slice-start = ((s8[5373952]{0:T(1024)(128)(4,1)}), s8[4194304]{0:T(1024)(128)(4,1)S(1)}, s32[]{:S(2)}) async-start(s8[5373952]{0:T(1024)(128)(4,1)} %bitcast.183), calls=%async_computation.20 | async-start | bytes 8388608
  288.1 177.2 %reduce-scatter.7.cloned.1.call-start = ((), (), s32[]{:S(2)}) async-start(), calls=%async_computation.15 | async-start | bytes 1572864 | tf_op jit(solution)/shard_map/reduce_scatter | solution.py:584
  315.6 149.7 %reduce-scatter.11.cloned.1.call-start = ((), (), s32[]{:S(2)}) async-start(), calls=%async_computation.17 | async-start | bytes 4030464 | tf_op jit(solution)/shard_map/reduce_scatter | solution.py:584
  320.1 145.2 %reduce-scatter.9.cloned.1.call-start = ((), (), s32[]{:S(2)}) async-start(), calls=%async_computation.16 | async-start | bytes 8060928 | tf_op jit(solution)/shard_map/reduce_scatter | solution.py:584
  328.2 170.7 %reduce-scatter.5.cloned.1.call-start = ((), (), s32[]{:S(2)}) async-start(), calls=%async_computation.14 | async-start | bytes 4718592 | tf_op jit(solution)/shard_map/reduce_scatter | solution.py:584
  456.3 66.9 %all-reduce.19.cloned.1.call-start = ((), (), s32[]{:S(2)}) async-start(), calls=%async_computation.19 | async-start | bytes 4194304 | tf_op jit(solution)/shard_map/psum | solution.py:541
  457.6 4.7 copy-start.18
  457.6 4.7 copy-start.19
  457.6 4.7 copy-start.21
  457.6 4.7 copy-start.24
  465.2 275.7 %all-reduce.17.cloned.1.call-start = ((), (), s32[]{:S(2)}) async-start(), calls=%async_computation.18 | async-start | bytes 12255232 | tf_op jit(solution)/shard_map/psum | solution.py:587
  740.9 4.8 copy-start.8
  (19 other events, 41.6 us)
Sparse Core Ops, SparseCore 0:
  10.2 47.6 all-gather.6
  74.1 21.7 all-gather.8
  97.5 39.7 all-gather.12
  178.1 17.7 all-reduce.12
  197.3 71.2 all-gather.10
  288.2 19.5 all-reduce.14
  315.7 21.4 reduce-scatter.6
  339.6 38.2 reduce-scatter.10
  380.8 67.1 reduce-scatter.8
  456.5 42.4 reduce-scatter.4
  501.9 21.2 all-reduce.18
  528.5 212.2 all-reduce.16

commit v2 on v1

--- a/solution.py
+++ b/solution.py
@@ -492,6 +492,41 @@
     return lax.all_to_all(array_in, "ctx", split_axis=0, concat_axis=0, tiled=True)
 
 
+def swapped(array_in, axis):
+    return lax.ppermute(array_in, axis, [(0, 1), (1, 0)])
+
+
+def gathered(block, dimension):
+    if lax.axis_size("shard") != 2:
+        return lax.all_gather(block, "shard", axis=dimension, tiled=True)
+    other = swapped(block, "shard")
+    return jnp.where(
+        lax.axis_index("shard") == 0,
+        jnp.concatenate([block, other], axis=dimension),
+        jnp.concatenate([other, block], axis=dimension),
+    )
+
+
+def core_sum(partial):
+    low = partial.astype(jnp.bfloat16)
+    if lax.axis_size("tp") != 2:
+        return lax.psum(low, "tp").astype(jnp.float32)
+    return low.astype(jnp.float32) + swapped(low, "tp").astype(jnp.float32)
+
+
+def owned_partial(product, cut, dimension, cut_axis):
+    if lax.axis_size("shard") != 2:
+        return lax.psum_scatter(
+            product(cut).astype(jnp.bfloat16), "shard", scatter_dimension=dimension, tiled=True
+        )
+    half = cut.shape[cut_axis] // 2
+    place = lax.axis_index("shard")
+    theirs = lax.dynamic_slice_in_dim(cut, (1 - place) * half, half, cut_axis)
+    mine = lax.dynamic_slice_in_dim(cut, place * half, half, cut_axis)
+    arrived = swapped(product(theirs).astype(jnp.bfloat16), "shard")
+    return (product(mine) + arrived.astype(jnp.float32)).astype(jnp.bfloat16)
+
+
 def head_shards(tokens, cotangent, lengths, g_attn, w_qkv, w_attn_out, g_mlp, w_in, w_mlp_out):
     tok_rows = tokens.shape[0]
     ctx_size = lax.axis_size("ctx")
@@ -501,11 +536,15 @@
     cos_t, sin_t = rope_tables_t(inside, HD)
     ends = jnp.cumsum(lengths, axis=1).astype(jnp.int32)
 
-    attn_gain, qkv_full = (
-        lax.all_gather(g_attn, "shard", axis=0, tiled=True),
-        lax.all_gather(w_qkv, "shard", axis=0, tiled=True),
-    )
-    out_full = lax.all_gather(w_attn_out, "shard", axis=1, tiled=True)
+    attn_gain = gathered(g_attn, 0)
+    mlp_gain = gathered(g_mlp, 0)
+    qkv_full = gathered(w_qkv, 0)
+    w_in, w_mlp_out, w_attn_out, qkv_full = lax.optimization_barrier(
+        (w_in, w_mlp_out, w_attn_out, qkv_full)
+    )
+    out_full = gathered(w_attn_out, 1)
+    in_full = gathered(w_in, 0)
+    down_full = gathered(w_mlp_out, 1)
     residual = tokens.astype(jnp.float32)
     normed_one, norm_one_back = jax.vjp(layer_norm, residual, attn_gain.astype(jnp.float32))
     hidden_one = normed_one.astype(jnp.bfloat16)
@@ -524,42 +563,49 @@
     ).reshape(ctx_size, own_heads, 3 * HD, tok_rows)
     packed = exchanged(packed)
     own_low, own_attended, lse = attention_forward(ends, packed)
+    own_low, in_full, out_full = lax.optimization_barrier((own_low, in_full, out_full))
     attn_low = exchanged(own_low).reshape(local_width, tok_rows)
     attn_part = jnp.einsum("nt,nd->td", attn_low, out_full, preferred_element_type=jnp.float32)
-    middle = residual + lax.psum(attn_part.astype(jnp.bfloat16), "tp").astype(jnp.float32)
-    mlp_gain, in_full, down_full = (
-        lax.all_gather(g_mlp, "shard", axis=0, tiled=True),
-        lax.all_gather(w_in, "shard", axis=0, tiled=True),
-        lax.all_gather(w_mlp_out, "shard", axis=1, tiled=True),
-    )
+    middle = residual + core_sum(attn_part)
     normed_two, norm_two_back = jax.vjp(layer_norm, middle, mlp_gain.astype(jnp.float32))
     hidden_two = normed_two.astype(jnp.bfloat16)
     lifted = jnp.einsum("td,dcf->tcf", hidden_two, in_full, preferred_element_type=jnp.float32)
     mixed_f, geglu_back = jax.vjp(geglu, lifted)
     mixed_low = mixed_f.astype(jnp.bfloat16)
     mlp_part = jnp.dot(mixed_low, down_full, preferred_element_type=jnp.float32)
-    output = (middle + lax.psum(mlp_part.astype(jnp.bfloat16), "tp").astype(jnp.float32)).astype(
-        jnp.bfloat16
-    )
-    grad_down = jnp.einsum("tf,td->fd", mixed_low, cotangent, preferred_element_type=jnp.float32)
+    output = (middle + core_sum(mlp_part)).astype(jnp.bfloat16)
+    part_down = owned_partial(
+        lambda cut: jnp.einsum("tf,td->fd", mixed_low, cut, preferred_element_type=jnp.float32),
+        cotangent,
+        1,
+        1,
+    )
     grad_mixed = jnp.einsum("td,fd->tf", cotangent, down_full, preferred_element_type=jnp.float32)
     (grad_lifted,) = geglu_back(grad_mixed)
     lifted_low = grad_lifted.astype(jnp.bfloat16)
-    grad_in = jnp.einsum("td,tcf->dcf", hidden_two, lifted_low, preferred_element_type=jnp.float32)
+    part_in = owned_partial(
+        lambda cut: jnp.einsum("td,tcf->dcf", cut, lifted_low, preferred_element_type=jnp.float32),
+        hidden_two,
+        0,
+        1,
+    )
     hidden_two_part = jnp.einsum(
         "tcf,dcf->td", lifted_low, in_full, preferred_element_type=jnp.float32
     )
-    grad_hidden_two = lax.psum(hidden_two_part.astype(jnp.bfloat16), "tp").astype(jnp.float32)
-    grad_middle_norm, grad_mlp_gain = norm_two_back(grad_hidden_two)
+    grad_middle_norm, grad_mlp_gain = norm_two_back(core_sum(hidden_two_part))
     grad_middle = cotangent.astype(jnp.float32) + grad_middle_norm
     grad_branch = grad_middle.astype(jnp.bfloat16)
-    grad_attn_out = jnp.einsum(
-        "nt,td->nd", attn_low, grad_branch, preferred_element_type=jnp.float32
+    part_out = owned_partial(
+        lambda cut: jnp.einsum("nt,td->nd", attn_low, cut, preferred_element_type=jnp.float32),
+        grad_branch,
+        1,
+        1,
     )
     grad_attended = jnp.einsum(
         "td,nd->nt", grad_branch, out_full, preferred_element_type=jnp.float32
     ).astype(jnp.bfloat16)
     own_grads = exchanged(grad_attended.reshape(ctx_size, own_heads, HD, tok_rows))
+    summed_early = lax.psum((part_in, part_down, part_out), "ctx")
     own_packed = attention_backward(ends, packed, own_grads, own_attended, lse)
     grad_packed = exchanged(own_packed).reshape(head_count, 3, HD, tok_rows)
     grad_projected = jnp.stack(
@@ -570,31 +616,36 @@
         ],
         axis=0,
     ).reshape(3, local_width, tok_rows)
-    grad_qkv = jnp.einsum(
-        "td,cnt->dcn", hidden_one, grad_projected, preferred_element_type=jnp.float32
+    part_qkv = owned_partial(
+        lambda cut: jnp.einsum(
+            "td,cnt->dcn", cut, grad_projected, preferred_element_type=jnp.float32
+        ),
+        hidden_one,
+        0,
+        1,
     )
     hidden_one_part = jnp.einsum(
         "cnt,dcn->td", grad_projected, qkv_full, preferred_element_type=jnp.float32
     )
-    grad_hidden_one = lax.psum(hidden_one_part.astype(jnp.bfloat16), "tp").astype(jnp.float32)
-    grad_input_norm, grad_attn_gain = norm_one_back(grad_hidden_one)
+    grad_input_norm, grad_attn_gain = norm_one_back(core_sum(hidden_one_part))
     grad_tokens = (grad_middle + grad_input_norm).astype(jnp.bfloat16)
-
-    def owned(partial, dimension):
-        part = lax.psum_scatter(
-            partial.astype(jnp.bfloat16), "shard", scatter_dimension=dimension, tiled=True
-        )
-        return lax.psum(part, "ctx").astype(jnp.float32)
-
+    gains = lax.psum_scatter(
+        jnp.stack([grad_attn_gain, grad_mlp_gain]).astype(jnp.bfloat16),
+        "shard",
+        scatter_dimension=1,
+        tiled=True,
+    )
+    part_qkv, gains, summed_early = lax.optimization_barrier((part_qkv, gains, summed_early))
+    summed_qkv, gains = lax.psum((part_qkv, gains), "ctx")
     return (
         output,
         grad_tokens,
-        owned(grad_attn_gain, 0),
-        owned(grad_qkv, 0),
-        owned(grad_attn_out, 1),
-        owned(grad_mlp_gain, 0),
-        owned(grad_in, 0),
-        owned(grad_down, 1),
+        gains[0].astype(jnp.float32),
+        summed_qkv.astype(jnp.float32),
+        summed_early[2].astype(jnp.float32),
+        gains[1].astype(jnp.float32),
+        summed_early[0].astype(jnp.float32),
+        summed_early[1].astype(jnp.float32),
     )
 
 

time: 762 us -> 715 us (0.938)
  blocking collectives: 98.4 us -> 40.9 us
  waiting for transfers between devices: 428 us -> 408 us
  starting transfers between devices: 10.3 us -> 26.9 us
  other arithmetic: 40.5 us -> 55.3 us
    ppermute x0 -> x14, waiting for transfers between devices: none -> 183 us  [swapped(): return lax.ppermute(array_in, axis, [(0, 1), (1, 0)])]
    all_gather x4 -> x0, waiting for transfers between devices: 112 us -> none  [the longest x1 70.5 us: head_shards(): lax.all_gather(w_in, 'shard', axis=0, tiled=True)]
    psum x4 -> x2, waiting for transfers between devices: 231 us -> 185 us  [the longest x1 123 us: head_shards(): summed_early = lax.psum((part_in, part_down, part_out), 'ctx')]
    all_to_all x2 -> x1, blocking collectives: 61.2 us -> 20.6 us  [exchanged(): lax.all_to_all(array_in, 'ctx', split_axis=0, concat_axis=0, tiled=True)]
    reduce_scatter x4 -> x0, waiting for transfers between devices: 33.7 us -> none  [owned(): lax.psum_scatter(partial.astype(jnp.bfloat16), 'shard', scatter_dimension...]
    select_n x0 -> x3, other arithmetic: none -> 13 us  [gathered(): jnp.where(lax.axis_index('shard') == 0, jnp.concatenate([block, other], a...]
    ppermute x0 -> x14, starting transfers between devices: none -> 10.2 us  [swapped(): return lax.ppermute(array_in, axis, [(0, 1), (1, 0)])]
    all_to_all x2 -> x3, waiting for transfers between devices: 49.5 us -> 39.6 us  [exchanged(): lax.all_to_all(array_in, 'ctx', split_axis=0, concat_axis=0, tiled=True)]
  transfers between devices with their start and end apart: 14 -> 20, of which waited for: 9 -> 11; matrix products, arithmetic and copies ran while one was open for 7% -> 13% of each run, Pallas kernels for 13% -> 0%
where the time goes in v2:
time: 715 us; the launch traced here: 710 us
  waiting for transfers between devices  408 us (57%)
  Pallas kernels  98.2 us (14%)
  other arithmetic  55.3 us (8%)
  matrix products  52 us (7%)
  blocking collectives  40.9 us (6%)
  starting transfers between devices  26.9 us (4%)
  between operations  16.3 us (2%)
  local copies, waits for them, and re-layouts  12.2 us (2%)
    ppermute x14, waiting for transfers between devices, swapped(): return lax.ppermute(array_in, axis, [(0, 1), (1, 0)])  183 us
    psum x1, waiting for transfers between devices, head_shards(): summed_early = lax.psum((part_in, part_down, part_out), 'ctx')  123 us
    psum x1, waiting for transfers between devices, head_shards(): summed_qkv, gains = lax.psum((part_qkv, gains), 'ctx')  61.3 us
    pallas_call x1, Pallas kernels, attention_backward(): pl.pallas_call(functools.partial(backward_kernel, blocks), grid=(heads, b...  51.7 us
    pallas_call x1, Pallas kernels, attention_forward(): pl.pallas_call(functools.partial(forward_kernel, blocks), grid=(heads, bl...  46.5 us
    all_to_all x3, waiting for transfers between devices, exchanged(): lax.all_to_all(array_in, 'ctx', split_axis=0, concat_axis=0, tiled=True)  39.6 us
    all_to_all x1, blocking collectives, exchanged(): lax.all_to_all(array_in, 'ctx', split_axis=0, concat_axis=0, tiled=True)  20.6 us
    psum x1, blocking collectives, head_shards(): summed_qkv, gains = lax.psum((part_qkv, gains), 'ctx')  20.2 us
  transfers between devices with their start and end apart: 20, of which 11 were waited for; matrix products, arithmetic and copies ran while one was open for 13% of the time, Pallas kernels for 0%

profile of v2, /device:TPU:0, one launch (start us, length us, event | category | flops | bytes accessed | tf_op | source)
XLA Modules:
  0.0 709.9 jit_solution(10939315554293248305)
XLA Ops:
  17.4 29.8 %collective-permute-done = bf16[512,3,512]{2,0,1:T(8,128)(2,1)} collective-permute-done((bf16[512,3,512]{2,0,1:T(8,128)(2,1)}, bf16[512,3,512]{2,0,1:T(8,128)(2,1)}, u32[]{:S(2)}, u32[]{:S(2)}) %collective-permute-start) | collective-permute-done | bytes 1572896 | tf_op jit(solution)/shard_map/ppermute | solution.py:496
  54.0 6.1 all-to-all-start
  62.4 59.8 %collective-permute-done.3 = bf16[512,512]{1,0:T(8,128)(2,1)} collective-permute-done((bf16[512,512]{1,0:T(8,128)(2,1)S(1)}, bf16[512,512]{1,0:T(8,128)(2,1)}, u32[]{:S(2)}, u32[]{:S(2)}) %collective-permute-start.3) | collective-permute-done | bytes 524320 | tf_op jit(solution)/shard_map/ppermute | solution.py:496
  124.8 8.1 %maximum_select_fusion = bf16[1024,2,1312]{0,2,1:T(8,128)(2,1)} fusion(bf16[512,2,1312]{0,2,1:T(8,128)(2,1)} %collective-permute-done.2, bf16[512,2,1312]{0,2,1:T(8,128)(2,1)} %param.16, pred[]{:T(512)S(6)} %eq.8), kind=kLoop, calls=%fused_computation | loop fusion | flops 24182784 | bytes 10747905 | tf_op jit(solution)/shard_map/jit(_where)/select_n | solution.py:503
  134.0 46.5 %attention_forward.1 = (bf16[8,1,64,512]{3,2,1,0:T(8,128)(2,1)}, f32[8,1,64,512]{3,2,1,0:T(8,128)}, f32[8,1,1,512]{3,2,1,0:T(1,128)}) custom-call(s32[1,4]{1,0:T(1,128)} %reduce_window_sum.18.ends_ref, bf16[8,1,192,512]{3,2,1,0:T(8,128)(2,1)} %copy-done.16, bf16[8,1,192,512]{3,2,1,0:T(8,128)(2,1)} %copy-done.16, bf16[8,1,192,512]{3,2,1,0:T(8,128)(2,1)} %copy-done.16), custom_call_target="tpu_custom_call" | custom-call | flops 17179869184 | bytes 4718592 | tf_op jit(solution)/shard_map/attention_forward/pallas_call | solution.py:447
  180.5 6.2 all-to-all-start.1
  187.3 11.7 %all-to-all-done.1 = bf16[8,1,64,512]{3,2,1,0:T(8,128)(2,1)S(1)} async-done(((bf16[8,1,64,512]{3,2,1,0:T(8,128)(2,1)}), bf16[8,1,64,512]{3,2,1,0:T(8,128)(2,1)S(1)}, u32[]{:S(2)}, u32[]{:S(2)}) %all-to-all-start.1) | async-done | bytes 524320 | tf_op jit(solution)/shard_map/all_to_all | solution.py:492
  201.9 14.0 %collective-permute-done.5 = bf16[512]{0:T(512)(128)(2,1)S(1)} collective-permute-done((bf16[512]{0:T(512)(128)(2,1)S(1)}, bf16[512]{0:T(512)(128)(2,1)S(1)}, u32[]{:S(2)}, u32[]{:S(2)}) %collective-permute-start.5) | collective-permute-done | bytes 1056 | tf_op jit(solution)/shard_map/ppermute | solution.py:496
  223.7 6.2 multiply_bitcast_fusion
  245.7 20.6 %all_to_all.20.do_ref = bf16[8,1,64,512]{3,2,1,0:T(8,128)(2,1)} all-to-all(bf16[8,1,64,512]{3,2,1,0:T(8,128)(2,1)S(1)} %bitcast.186), channel_id=1, replica_groups=mesh['shard'=2,'ctx'=8,'tp'=2] {'ctx'}, dimensions={0} | all-to-all | bytes 1048576 | tf_op jit(solution)/shard_map/all_to_all | solution.py:492
  266.4 51.7 %attention_backward.1 = bf16[8,1,192,512]{3,2,1,0:T(8,128)(2,1)} custom-call(s32[1,4]{1,0:T(1,128)} %reduce_window_sum.18.ends_ref, bf16[8,1,192,512]{3,2,1,0:T(8,128)(2,1)} %copy-done.16, bf16[8,1,192,512]{3,2,1,0:T(8,128)(2,1)} %copy-done.16, bf16[8,1,192,512]{3,2,1,0:T(8,128)(2,1)} %copy-done.16, bf16[8,1,64,512]{3,2,1,0:T(8,128)(2,1)} %all_to_all.20.do_ref, ...), custom_call_target="tpu_custom_call" | custom-call | flops 42949672960 | bytes 7864320 | tf_op jit(solution)/shard_map/attention_backward/pallas_call | solution.py:471
  318.0 4.3 all-to-all-start.3
  331.2 27.9 %all-to-all-done.3 = bf16[8,1,192,512]{3,2,1,0:T(8,128)(2,1)} async-done(((bf16[8,1,192,512]{3,2,1,0:T(8,128)(2,1)}), bf16[8,1,192,512]{3,2,1,0:T(8,128)(2,1)}, u32[]{:S(2)}, u32[]{:S(2)}) %all-to-all-start.3) | async-done | bytes 1572896 | tf_op jit(solution)/shard_map/all_to_all | solution.py:492
  369.1 5.3 bitcast_convert_fusion
  376.2 4.0 add_convert_fusion.3
  380.2 45.6 %collective-permute-done.13 = bf16[512,512]{1,0:T(8,128)(2,1)} collective-permute-done((bf16[512,512]{1,0:T(8,128)(2,1)}, bf16[512,512]{1,0:T(8,128)(2,1)}, u32[]{:S(2)}, u32[]{:S(2)}) %collective-permute-start.13) | collective-permute-done | bytes 524320 | tf_op jit(solution)/shard_map/ppermute | solution.py:496
  434.0 6.6 add_convert_fusion
  440.6 3.7 convolution_convert_fusion.2
  446.8 32.4 %collective-permute-done.10 = bf16[512,3,512]{2,0,1:T(8,128)(2,1)} collective-permute-done((bf16[512,3,512]{2,0,1:T(8,128)(2,1)}, bf16[512,3,512]{2,0,1:T(8,128)(2,1)}, u32[]{:S(2)}, u32[]{:S(2)}) %collective-permute-start.10) | collective-permute-done | bytes 1572896 | tf_op jit(solution)/shard_map/ppermute | solution.py:496
  479.3 4.3 add_convert_fusion.2
  483.6 123.2 %all-reduce.8.cloned.1.call-done = (bf16[512,2,1312]{0,2,1:T(8,128)(2,1)}, bf16[1312,512]{1,0:T(8,128)(2,1)}, bf16[512,512]{1,0:T(8,128)(2,1)}) async-done(((bf16[512,2,1312]{0,2,1:T(8,128)(2,1)}, bf16[1312,512]{1,0:T(8,128)(2,1)}, bf16[512,512]{1,0:T(8,128)(2,1)}), (bf16[512,2,1312]{0,2,1:T(8,128)(2,1)}, bf16[1312,512]{1,0:T(8,128)(2,1)}, bf16[512,512]{1,0:T(8,128)(2,1)})) %all-reduce.8.cloned.1.call-update) | async-done | bytes 4554768 | tf_op jit(solution)/shard_map/psum | solution.py:608
  606.9 3.6 add_convert_fusion.4
  616.6 20.2 %psum.38 = bf16[2,512]{1,0:T(2,128)(2,1)S(1)} all-reduce(bf16[2,512]{1,0:T(2,128)(2,1)S(1)} %copy.73), channel_id=1, replica_groups=mesh['shard'=2,'ctx'=8,'tp'=2] {'ctx'}, use_global_device_ids=true, to_apply=%region_18.19 | all-reduce | flops 1024 | bytes 4096 | tf_op jit(solution)/shard_map/psum | solution.py:639
  637.4 61.3 %all-reduce.6.cloned.1.call-done = bf16[512,3,512]{2,0,1:T(8,128)(2,1)} async-done(((bf16[512,3,512]{2,0,1:T(8,128)(2,1)}), bf16[512,3,512]{2,0,1:T(8,128)(2,1)}) %all-reduce.6.cloned.1.call-update) | async-done | bytes 1572880 | tf_op jit(solution)/shard_map/psum | solution.py:639
  (163 shorter events, 90.4 us)
Async XLA Ops:
  8.0 39.2 %copy-start.17 = (bf16[512,3,512]{2,0,1:T(8,128)(2,1)S(1)}, bf16[512,3,512]{2,0,1:T(8,128)(2,1)}, u32[]{:S(2)}) copy-start(bf16[512,3,512]{2,0,1:T(8,128)(2,1)} %param.13) | copy-start | bytes 4718596
  8.0 8.2 %collective-permute-start.1 = (bf16[512]{0:T(512)(128)(2,1)}, bf16[512]{0:T(512)(128)(2,1)S(1)}, u32[]{:S(2)}, u32[]{:S(2)}) collective-permute-start(bf16[512]{0:T(512)(128)(2,1)} %param.12), channel_id=1, source_target_pairs={{0,16},{16,0},{1,17},{17,1},{2,18},{18,2},{3,19},{19,3},{4,20},{20... | collective-permute-start | bytes 3080 | tf_op jit(solution)/shard_map/ppermute | solution.py:496
  11.1 36.2 %collective-permute-start = (bf16[512,3,512]{2,0,1:T(8,128)(2,1)}, bf16[512,3,512]{2,0,1:T(8,128)(2,1)}, u32[]{:S(2)}, u32[]{:S(2)}) collective-permute-start(bf16[512,3,512]{2,0,1:T(8,128)(2,1)} %param.13), channel_id=1, source_target_pairs={{0,16},{16,0},{1,17},{17,1},{2,18},{18,2},{3,19},{19,3},{4,20},{20... | collective-permute-start | bytes 4718600 | tf_op jit(solution)/shard_map/ppermute | solution.py:496
  51.8 72.9 %collective-permute-start.2 = (bf16[512,2,1312]{0,2,1:T(8,128)(2,1)}, bf16[512,2,1312]{0,2,1:T(8,128)(2,1)}, u32[]{:S(2)}, u32[]{:S(2)}) collective-permute-start(bf16[512,2,1312]{0,2,1:T(8,128)(2,1)} %param.16), channel_id=1, source_target_pairs={{0,16},{16,0},{1,17},{17,1},{2,18},{18,2},{3,19},{19,3},{4,20},{20... | collective-permute-start | bytes 8060936 | tf_op jit(solution)/shard_map/ppermute | solution.py:496
  54.0 78.8 %all-to-all-start = ((bf16[8,1,192,512]{3,2,1,0:T(8,128)(2,1)}), bf16[8,1,192,512]{3,2,1,0:T(8,128)(2,1)S(1)}, u32[]{:S(2)}, u32[]{:S(2)}) async-start(bf16[8,1,192,512]{3,2,1,0:T(8,128)(2,1)} %bitcast.180), calls=%async_computation | async-start | bytes 3145728 | tf_op jit(solution)/shard_map/all_to_all | solution.py:492
  60.2 62.1 %collective-permute-start.3 = (bf16[512,512]{1,0:T(8,128)(2,1)S(1)}, bf16[512,512]{1,0:T(8,128)(2,1)}, u32[]{:S(2)}, u32[]{:S(2)}) collective-permute-start(bf16[512,512]{1,0:T(8,128)(2,1)S(1)} %copy-done.24), channel_id=1, source_target_pairs={{0,16},{16,0},{1,17},{17,1},{2,18},{18,2},{3,19},{19,3},{4,20},{20... | collective-permute-start | bytes 1572872 | tf_op jit(solution)/shard_map/ppermute | solution.py:496
  180.5 35.5 %copy-start.7 = (bf16[512,1024]{1,0:T(8,128)(2,1)S(1)}, bf16[512,1024]{1,0:T(8,128)(2,1)}, u32[]{:S(2)}) copy-start(bf16[512,1024]{1,0:T(8,128)(2,1)} %param.10) | copy-start | bytes 3145732
  180.5 18.5 %all-to-all-start.1 = ((bf16[8,1,64,512]{3,2,1,0:T(8,128)(2,1)}), bf16[8,1,64,512]{3,2,1,0:T(8,128)(2,1)S(1)}, u32[]{:S(2)}, u32[]{:S(2)}) async-start(bf16[8,1,64,512]{3,2,1,0:T(8,128)(2,1)} %get-tuple-element.27), calls=%async_computation.1 | async-start | bytes 1048576 | tf_op jit(solution)/shard_map/all_to_all | solution.py:492
  186.7 29.2 %collective-permute-start.6 = (bf16[1312,512]{1,0:T(8,128)(2,1)}, bf16[1312,512]{1,0:T(8,128)(2,1)}, u32[]{:S(2)}, u32[]{:S(2)}) collective-permute-start(bf16[1312,512]{1,0:T(8,128)(2,1)} %param.17), channel_id=1, source_target_pairs={{0,16},{16,0},{1,17},{17,1},{2,18},{18,2},{3,19},{19,3},{4,20},{20... | collective-permute-start | bytes 4030472 | tf_op jit(solution)/shard_map/ppermute | solution.py:496
  201.2 18.2 %collective-permute-start.4 = (bf16[512,1024]{1,0:T(8,128)(2,1)S(1)}, bf16[512,1024]{1,0:T(8,128)(2,1)S(1)}, u32[]{:S(2)}, u32[]{:S(2)}) collective-permute-start(bf16[512,1024]{1,0:T(8,128)(2,1)S(1)} %convolution_convert_fusion.4), channel_id=1, source_target_pairs={{0,1},{1,0},{2,3},{3,2},{4,5},{5,4},{6,7},{7,6},{8,9},{9,8},{10,11... | collective-permute-start | bytes 3145736 | tf_op jit(solution)/shard_map/ppermute | solution.py:496
  201.3 14.6 %collective-permute-start.5 = (bf16[512]{0:T(512)(128)(2,1)S(1)}, bf16[512]{0:T(512)(128)(2,1)S(1)}, u32[]{:S(2)}, u32[]{:S(2)}) collective-permute-start(bf16[512]{0:T(512)(128)(2,1)S(1)} %copy-done.26), channel_id=1, source_target_pairs={{0,16},{16,0},{1,17},{17,1},{2,18},{18,2},{3,19},{19,3},{4,20},{20... | collective-permute-start | bytes 3080 | tf_op jit(solution)/shard_map/ppermute | solution.py:496
  235.1 4.2 collective-permute-start.8
  238.7 2.8 collective-permute-start.7
  318.0 41.0 %all-to-all-start.3 = ((bf16[8,1,192,512]{3,2,1,0:T(8,128)(2,1)}), bf16[8,1,192,512]{3,2,1,0:T(8,128)(2,1)}, u32[]{:S(2)}, u32[]{:S(2)}) async-start(bf16[8,1,192,512]{3,2,1,0:T(8,128)(2,1)} %attention_backward.1), calls=%async_computation.3 | async-start | bytes 3145728 | tf_op jit(solution)/shard_map/all_to_all | solution.py:492
  322.4 123.4 %reduce-scatter.4.cloned.1.call-start = ((), (), s32[]{:S(2)}) async-start(), calls=%async_computation.6 | async-start | bytes 393216
  326.0 50.2 %collective-permute-start.12 = (bf16[1312,512]{1,0:T(8,128)(2,1)}, bf16[1312,512]{1,0:T(8,128)(2,1)}, u32[]{:S(2)}, u32[]{:S(2)}) collective-permute-start(bf16[1312,512]{1,0:T(8,128)(2,1)} %convolution_convert_fusion.1), channel_id=1, source_target_pairs={{0,16},{16,0},{1,17},{17,1},{2,18},{18,2},{3,19},{19,3},{4,20},{20... | collective-permute-start | bytes 4030472 | tf_op jit(solution)/shard_map/ppermute | solution.py:496
  329.7 104.3 %collective-permute-start.11 = (bf16[512,2,1312]{0,2,1:T(8,128)(2,1)}, bf16[512,2,1312]{0,2,1:T(8,128)(2,1)}, u32[]{:S(2)}, u32[]{:S(2)}) collective-permute-start(bf16[512,2,1312]{0,2,1:T(8,128)(2,1)} %convolution_convert_fusion), channel_id=1, source_target_pairs={{0,16},{16,0},{1,17},{17,1},{2,18},{18,2},{3,19},{19,3},{4,20},{20... | collective-permute-start | bytes 8060936 | tf_op jit(solution)/shard_map/ppermute | solution.py:496
  374.4 53.7 %collective-permute-start.9 = (bf16[512,1024]{1,0:T(8,128)(2,1)}, bf16[512,1024]{1,0:T(8,128)(2,1)}, u32[]{:S(2)}, u32[]{:S(2)}) collective-permute-start(bf16[512,1024]{1,0:T(8,128)(2,1)} %bitcast_convert_fusion), channel_id=1, source_target_pairs={{0,1},{1,0},{2,3},{3,2},{4,5},{5,4},{6,7},{7,6},{8,9},{9,8},{10,11... | collective-permute-start | bytes 3145736 | tf_op jit(solution)/shard_map/ppermute | solution.py:496
  375.6 50.1 %collective-permute-start.13 = (bf16[512,512]{1,0:T(8,128)(2,1)}, bf16[512,512]{1,0:T(8,128)(2,1)}, u32[]{:S(2)}, u32[]{:S(2)}) collective-permute-start(bf16[512,512]{1,0:T(8,128)(2,1)} %convolution_convert_fusion.5), channel_id=1, source_target_pairs={{0,16},{16,0},{1,17},{17,1},{2,18},{18,2},{3,19},{19,3},{4,20},{20... | collective-permute-start | bytes 1572872 | tf_op jit(solution)/shard_map/ppermute | solution.py:496
  376.2 49.6 %copy-start.3 = (bf16[8,1,64,512]{3,2,1,0:T(8,128)(2,1)S(1)}, bf16[8,1,64,512]{3,2,1,0:T(8,128)(2,1)}, u32[]{:S(2)}) copy-start(bf16[8,1,64,512]{3,2,1,0:T(8,128)(2,1)} %copy-done.1) | copy-start | bytes 1572868
  376.2 49.6 %copy-start.6 = (bf16[512,1024]{1,0:T(8,128)(2,1)S(1)}, bf16[512,1024]{1,0:T(8,128)(2,1)}, u32[]{:S(2)}) copy-start(bf16[512,1024]{1,0:T(8,128)(2,1)} %copy-done.4) | copy-start | bytes 3145732
  433.9 172.9 %all-reduce.8.cloned.1.call-start = ((), (), s32[]{:S(2)}) async-start(), calls=%async_computation.7 | async-start | bytes 9109504 | tf_op jit(solution)/shard_map/psum | solution.py:608
  440.6 258.1 %all-reduce.6.cloned.1.call-start = ((), (), s32[]{:S(2)}) async-start(), calls=%async_computation.5 | async-start | bytes 3145728 | tf_op jit(solution)/shard_map/psum | solution.py:639
  444.3 35.0 %collective-permute-start.10 = (bf16[512,3,512]{2,0,1:T(8,128)(2,1)}, bf16[512,3,512]{2,0,1:T(8,128)(2,1)}, u32[]{:S(2)}, u32[]{:S(2)}) collective-permute-start(bf16[512,3,512]{2,0,1:T(8,128)(2,1)} %convolution_convert_fusion.2), channel_id=1, source_target_pairs={{0,16},{16,0},{1,17},{17,1},{2,18},{18,2},{3,19},{19,3},{4,20},{20... | collective-permute-start | bytes 4718600 | tf_op jit(solution)/shard_map/ppermute | solution.py:496
  (28 other events, 182.5 us)
Sparse Core Ops, SparseCore 0:
  434.0 11.7 reduce-scatter.3
Sparse Core Ops, SparseCore 1:
  440.7 166.1 all-reduce.7
  610.6 88.0 all-reduce.5

commit v3 on v1

--- a/solution.py
+++ b/solution.py
@@ -295,6 +295,7 @@
 
 
 LOG2E = 1.4426950408889634
+RING = [0, 2, 4, 6, 7, 5, 3, 1]
 VMEM_BYTES = 56 * 1024 * 1024
 
 
@@ -492,6 +493,62 @@
     return lax.all_to_all(array_in, "ctx", split_axis=0, concat_axis=0, tiled=True)
 
 
+def swapped(array_in, axis):
+    return lax.ppermute(array_in, axis, [(0, 1), (1, 0)])
+
+
+def joined(block, other, dimension):
+    return jnp.where(
+        lax.axis_index("shard") == 0,
+        jnp.concatenate([block, other], axis=dimension),
+        jnp.concatenate([other, block], axis=dimension),
+    )
+
+
+def halves(array_in, axis):
+    half = array_in.shape[axis] // 2
+    place = lax.axis_index("shard")
+    return (
+        lax.dynamic_slice_in_dim(array_in, place * half, half, axis),
+        lax.dynamic_slice_in_dim(array_in, (1 - place) * half, half, axis),
+    )
+
+
+def added(product, arrived):
+    return (product + arrived.astype(jnp.float32)).astype(jnp.bfloat16)
+
+
+def core_sum(partial):
+    low = partial.astype(jnp.bfloat16)
+    return low.astype(jnp.float32) + swapped(low, "tp").astype(jnp.float32)
+
+
+def block_sum(partial):
+    size = lax.axis_size("ctx")
+    place = lax.axis_index("ctx")
+    pieces = exchanged(partial)
+    total = jnp.sum(pieces.astype(jnp.float32), axis=0).astype(jnp.bfloat16)
+    order = RING if size == len(RING) else list(range(size))
+    spots = [0] * size
+    for i in range(size):
+        spots[order[i]] = i
+    spot = jnp.array(spots, jnp.int32)[place]
+    ring = jnp.array(order, jnp.int32)
+    result = jnp.zeros((size,) + total.shape, jnp.bfloat16)
+    result = lax.dynamic_update_slice_in_dim(result, total[None], place, 0)
+    right, left = total, total
+    for step in range(1, size // 2 + 1):
+        forward = [(order[i], order[(i + 1) % size]) for i in range(size)]
+        right = lax.ppermute(right, "ctx", forward)
+        source = ring[(spot - step) % size]
+        result = lax.dynamic_update_slice_in_dim(result, right[None], source, 0)
+        if step < size - step:
+            left = lax.ppermute(left, "ctx", [(d, s) for s, d in forward])
+            source = ring[(spot + step) % size]
+            result = lax.dynamic_update_slice_in_dim(result, left[None], source, 0)
+    return result
+
+
 def head_shards(tokens, cotangent, lengths, g_attn, w_qkv, w_attn_out, g_mlp, w_in, w_mlp_out):
     tok_rows = tokens.shape[0]
     ctx_size = lax.axis_size("ctx")
@@ -501,11 +558,16 @@
     cos_t, sin_t = rope_tables_t(inside, HD)
     ends = jnp.cumsum(lengths, axis=1).astype(jnp.int32)
 
-    attn_gain, qkv_full = (
-        lax.all_gather(g_attn, "shard", axis=0, tiled=True),
-        lax.all_gather(w_qkv, "shard", axis=0, tiled=True),
-    )
-    out_full = lax.all_gather(w_attn_out, "shard", axis=1, tiled=True)
+    attn_gain = joined(g_attn, swapped(g_attn, "shard"), 0)
+    mlp_gain = joined(g_mlp, swapped(g_mlp, "shard"), 0)
+    qkv_other = swapped(w_qkv, "shard")
+    w_in, w_mlp_out, w_attn_out, qkv_other = lax.optimization_barrier(
+        (w_in, w_mlp_out, w_attn_out, qkv_other)
+    )
+    qkv_full = joined(w_qkv, qkv_other, 0)
+    out_other = swapped(w_attn_out, "shard")
+    in_other = swapped(w_in, "shard")
+    down_other = swapped(w_mlp_out, "shard")
     residual = tokens.astype(jnp.float32)
     normed_one, norm_one_back = jax.vjp(layer_norm, residual, attn_gain.astype(jnp.float32))
     hidden_one = normed_one.astype(jnp.bfloat16)
@@ -524,43 +586,67 @@
     ).reshape(ctx_size, own_heads, 3 * HD, tok_rows)
     packed = exchanged(packed)
     own_low, own_attended, lse = attention_forward(ends, packed)
+    own_low, in_other, out_other = lax.optimization_barrier((own_low, in_other, out_other))
+    out_full = joined(w_attn_out, out_other, 1)
+    in_full = joined(w_in, in_other, 0)
+    down_full = joined(w_mlp_out, down_other, 1)
     attn_low = exchanged(own_low).reshape(local_width, tok_rows)
     attn_part = jnp.einsum("nt,nd->td", attn_low, out_full, preferred_element_type=jnp.float32)
-    middle = residual + lax.psum(attn_part.astype(jnp.bfloat16), "tp").astype(jnp.float32)
-    mlp_gain, in_full, down_full = (
-        lax.all_gather(g_mlp, "shard", axis=0, tiled=True),
-        lax.all_gather(w_in, "shard", axis=0, tiled=True),
-        lax.all_gather(w_mlp_out, "shard", axis=1, tiled=True),
-    )
+    middle = residual + core_sum(attn_part)
     normed_two, norm_two_back = jax.vjp(layer_norm, middle, mlp_gain.astype(jnp.float32))
     hidden_two = normed_two.astype(jnp.bfloat16)
     lifted = jnp.einsum("td,dcf->tcf", hidden_two, in_full, preferred_element_type=jnp.float32)
     mixed_f, geglu_back = jax.vjp(geglu, lifted)
     mixed_low = mixed_f.astype(jnp.bfloat16)
     mlp_part = jnp.dot(mixed_low, down_full, preferred_element_type=jnp.float32)
-    output = (middle + lax.psum(mlp_part.astype(jnp.bfloat16), "tp").astype(jnp.float32)).astype(
-        jnp.bfloat16
-    )
-    grad_down = jnp.einsum("tf,td->fd", mixed_low, cotangent, preferred_element_type=jnp.float32)
+    output = (middle + core_sum(mlp_part)).astype(jnp.bfloat16)
+    def down_product(cut):
+        return jnp.einsum("tf,td->fd", mixed_low, cut, preferred_element_type=jnp.float32)
+
+    cot_mine, cot_theirs = halves(cotangent, 1)
+    send_down = down_product(cot_theirs).astype(jnp.bfloat16)
     grad_mixed = jnp.einsum("td,fd->tf", cotangent, down_full, preferred_element_type=jnp.float32)
     (grad_lifted,) = geglu_back(grad_mixed)
     lifted_low = grad_lifted.astype(jnp.bfloat16)
-    grad_in = jnp.einsum("td,tcf->dcf", hidden_two, lifted_low, preferred_element_type=jnp.float32)
+
+    def in_product(cut):
+        return jnp.einsum("td,tcf->dcf", cut, lifted_low, preferred_element_type=jnp.float32)
+
+    hidden_mine, hidden_theirs = halves(hidden_two, 1)
+    send_in = in_product(hidden_theirs).astype(jnp.bfloat16)
     hidden_two_part = jnp.einsum(
         "tcf,dcf->td", lifted_low, in_full, preferred_element_type=jnp.float32
     )
-    grad_hidden_two = lax.psum(hidden_two_part.astype(jnp.bfloat16), "tp").astype(jnp.float32)
-    grad_middle_norm, grad_mlp_gain = norm_two_back(grad_hidden_two)
+    grad_middle_norm, grad_mlp_gain = norm_two_back(core_sum(hidden_two_part))
     grad_middle = cotangent.astype(jnp.float32) + grad_middle_norm
     grad_branch = grad_middle.astype(jnp.bfloat16)
-    grad_attn_out = jnp.einsum(
-        "nt,td->nd", attn_low, grad_branch, preferred_element_type=jnp.float32
-    )
+
+    def out_product(cut):
+        return jnp.einsum("nt,td->nd", attn_low, cut, preferred_element_type=jnp.float32)
+
+    branch_mine, branch_theirs = halves(grad_branch, 1)
+    send_out = out_product(branch_theirs).astype(jnp.bfloat16)
     grad_attended = jnp.einsum(
         "td,nd->nt", grad_branch, out_full, preferred_element_type=jnp.float32
     ).astype(jnp.bfloat16)
+    grad_attended, send_down, send_in, send_out = lax.optimization_barrier(
+        (grad_attended, send_down, send_in, send_out)
+    )
+    down_arrived = swapped(send_down, "shard")
+    in_arrived = swapped(send_in, "shard")
+    out_arrived = swapped(send_out, "shard")
     own_grads = exchanged(grad_attended.reshape(ctx_size, own_heads, HD, tok_rows))
     own_packed = attention_backward(ends, packed, own_grads, own_attended, lse)
+    own_packed, down_arrived, in_arrived, out_arrived = lax.optimization_barrier(
+        (own_packed, down_arrived, in_arrived, out_arrived)
+    )
+    part_down = added(down_product(cot_mine), down_arrived)
+    part_in = added(in_product(hidden_mine), in_arrived)
+    part_out = added(out_product(branch_mine), out_arrived)
+    own_packed, part_down, part_in, part_out = lax.optimization_barrier(
+        (own_packed, part_down, part_in, part_out)
+    )
+    summed_early = lax.psum((part_in, part_down, part_out), "ctx")
     grad_packed = exchanged(own_packed).reshape(head_count, 3, HD, tok_rows)
     grad_projected = jnp.stack(
         [
@@ -570,37 +656,43 @@
         ],
         axis=0,
     ).reshape(3, local_width, tok_rows)
-    grad_qkv = jnp.einsum(
-        "td,cnt->dcn", hidden_one, grad_projected, preferred_element_type=jnp.float32
-    )
+
+    def qkv_product(cut):
+        return jnp.einsum("td,cnt->dcn", cut, grad_projected, preferred_element_type=jnp.float32)
+
+    one_mine, one_theirs = halves(hidden_one, 1)
+    qkv_arrived = swapped(qkv_product(one_theirs).astype(jnp.bfloat16), "shard")
     hidden_one_part = jnp.einsum(
         "cnt,dcn->td", grad_projected, qkv_full, preferred_element_type=jnp.float32
     )
-    grad_hidden_one = lax.psum(hidden_one_part.astype(jnp.bfloat16), "tp").astype(jnp.float32)
-    grad_input_norm, grad_attn_gain = norm_one_back(grad_hidden_one)
+    grad_input_norm, grad_attn_gain = norm_one_back(core_sum(hidden_one_part))
     grad_tokens = (grad_middle + grad_input_norm).astype(jnp.bfloat16)
-
-    def owned(partial, dimension):
-        part = lax.psum_scatter(
-            partial.astype(jnp.bfloat16), "shard", scatter_dimension=dimension, tiled=True
-        )
-        return lax.psum(part, "ctx").astype(jnp.float32)
-
+    gains_mine, gains_theirs = halves(jnp.stack([grad_attn_gain, grad_mlp_gain]), 1)
+    gains = added(gains_mine, swapped(gains_theirs.astype(jnp.bfloat16), "shard"))
+    part_qkv = added(qkv_product(one_mine), qkv_arrived)
+    own_rows = part_qkv.shape[0]
+    wide = part_qkv.reshape(ctx_size, own_rows // ctx_size, -1)
+    extra = gains.reshape(ctx_size, 1, -1)
+    extra = jnp.pad(extra, ((0, 0), (0, 15), (0, wide.shape[2] - extra.shape[2])))
+    summed = block_sum(jnp.concatenate([wide, extra], axis=1))
+    summed_qkv = summed[:, : wide.shape[1]].reshape(part_qkv.shape)
+    gains = summed[:, wide.shape[1], : gains.size // ctx_size].reshape(gains.shape)
     return (
         output,
         grad_tokens,
-        owned(grad_attn_gain, 0),
-        owned(grad_qkv, 0),
-        owned(grad_attn_out, 1),
-        owned(grad_mlp_gain, 0),
-        owned(grad_in, 0),
-        owned(grad_down, 1),
+        gains[0].astype(jnp.float32),
+        summed_qkv.astype(jnp.float32),
+        summed_early[2].astype(jnp.float32),
+        gains[1].astype(jnp.float32),
+        summed_early[0].astype(jnp.float32),
+        summed_early[1].astype(jnp.float32),
     )
 
 
 def layer(tokens, cotangent, lengths, g_attn, w_qkv, w_attn_out, g_mlp, w_in, w_mlp_out):
     head_count = w_qkv.shape[2] // HD
     whole_heads = head_count % lax.axis_size("ctx") == 0
+    whole_heads = whole_heads and lax.axis_size("shard") == 2 and lax.axis_size("tp") == 2
     return (head_shards if whole_heads else shards)(
         tokens, cotangent, lengths, g_attn, w_qkv, w_attn_out, g_mlp, w_in, w_mlp_out
     )

time: 762 us -> 650 us (0.85)
  waiting for transfers between devices: 428 us -> 295 us
  blocking collectives: 98.4 us -> 41.4 us
  starting transfers between devices: 10.3 us -> 38.2 us
  between operations: 15.4 us -> 33.5 us
  local copies, waits for them, and re-layouts: 16.7 us -> 28.9 us
  matrix products: 50.1 us -> 61.1 us
  other arithmetic: 40.5 us -> 48.4 us
    ppermute x0 -> x22, waiting for transfers between devices: none -> 131 us  [the longest x15 111 us: swapped(): return lax.ppermute(array_in, axis, [(0, 1), (1, 0)])]
    psum x4 -> x1, waiting for transfers between devices: 231 us -> 108 us  [head_shards(): summed_early = lax.psum((part_in, part_down, part_out), 'ctx')]
    all_gather x4 -> x0, waiting for transfers between devices: 112 us -> none  [the longest x1 70.5 us: head_shards(): lax.all_gather(w_in, 'shard', axis=0, tiled=True)]
    reduce_scatter x4 -> x0, waiting for transfers between devices: 33.7 us -> none  [owned(): lax.psum_scatter(partial.astype(jnp.bfloat16), 'shard', scatter_dimension...]
    psum x1 -> x0, blocking collectives: 22.4 us -> none  [owned(): return lax.psum(part, 'ctx').astype(jnp.float32)]
    all_to_all x2 -> x1, blocking collectives: 61.2 us -> 41.4 us  [exchanged(): lax.all_to_all(array_in, 'ctx', split_axis=0, concat_axis=0, tiled=True)]
    ppermute x0 -> x22, starting transfers between devices: none -> 17.8 us  [the longest x15 11.4 us: swapped(): return lax.ppermute(array_in, axis, [(0, 1), (1, 0)])]
    all_to_all x2 -> x4, starting transfers between devices: 9.23 us -> 20.4 us  [exchanged(): lax.all_to_all(array_in, 'ctx', split_axis=0, concat_axis=0, tiled=True)]
  transfers between devices with their start and end apart: 14 -> 27, of which waited for: 9 -> 13; matrix products, arithmetic and copies ran while one was open for 7% -> 10% of each run, Pallas kernels for 13% -> 15%
where the time goes in v3:
time: 650 us; the launch traced here: 645 us
  waiting for transfers between devices  295 us (45%)
  Pallas kernels  98.3 us (15%)
  matrix products  61.1 us (9%)
  other arithmetic  48.4 us (7%)
  blocking collectives  41.4 us (6%)
  starting transfers between devices  38.2 us (6%)
  between operations  33.5 us (5%)
  local copies, waits for them, and re-layouts  28.9 us (4%)
    ppermute x15, waiting for transfers between devices, swapped(): return lax.ppermute(array_in, axis, [(0, 1), (1, 0)])  111 us
    psum x1, waiting for transfers between devices, head_shards(): summed_early = lax.psum((part_in, part_down, part_out), 'ctx')  108 us
    all_to_all x4, waiting for transfers between devices, exchanged(): lax.all_to_all(array_in, 'ctx', split_axis=0, concat_axis=0, tiled=True)  55.4 us
    pallas_call x1, Pallas kernels, attention_backward(): pl.pallas_call(functools.partial(backward_kernel, blocks), grid=(heads, b...  51.8 us
    pallas_call x1, Pallas kernels, attention_forward(): pl.pallas_call(functools.partial(forward_kernel, blocks), grid=(heads, bl...  46.5 us
    all_to_all x1, blocking collectives, exchanged(): lax.all_to_all(array_in, 'ctx', split_axis=0, concat_axis=0, tiled=True)  41.4 us
    ppermute x4, waiting for transfers between devices, block_sum(): right = lax.ppermute(right, 'ctx', forward)  20.6 us
    all_to_all x4, starting transfers between devices, exchanged(): lax.all_to_all(array_in, 'ctx', split_axis=0, concat_axis=0, tiled=True)  20.4 us
  transfers between devices with their start and end apart: 27, of which 13 were waited for; matrix products, arithmetic and copies ran while one was open for 10% of the time, Pallas kernels for 15%

profile of v3, /device:TPU:0, one launch (start us, length us, event | category | flops | bytes accessed | tf_op | source)
XLA Modules:
  0.0 645.0 jit_solution(1330774843810508510)
XLA Ops:
  16.6 29.8 %collective-permute-done = bf16[512,3,512]{2,0,1:T(8,128)(2,1)} collective-permute-done((bf16[512,3,512]{2,0,1:T(8,128)(2,1)}, bf16[512,3,512]{2,0,1:T(8,128)(2,1)}, u32[]{:S(2)}, u32[]{:S(2)}) %collective-permute-start) | collective-permute-done | bytes 1572896 | tf_op jit(solution)/shard_map/ppermute | solution.py:497
  52.5 6.0 all-to-all-start
  61.3 33.1 %all-to-all-done.q_ref.k_ref.v_ref = bf16[8,1,192,512]{3,2,1,0:T(8,128)(2,1)S(1)} async-done(((bf16[8,1,192,512]{3,2,1,0:T(8,128)(2,1)}), bf16[8,1,192,512]{3,2,1,0:T(8,128)(2,1)S(1)}, u32[]{:S(2)}, u32[]{:S(2)}) %all-to-all-start) | async-done | bytes 1572896 | tf_op jit(solution)/shard_map/all_to_all | solution.py:493
  95.6 46.5 %attention_forward.1 = (bf16[8,1,64,512]{3,2,1,0:T(8,128)(2,1)}, f32[8,1,64,512]{3,2,1,0:T(8,128)}, f32[8,1,1,512]{3,2,1,0:T(1,128)}) custom-call(s32[1,4]{1,0:T(1,128)} %reduce_window_sum.18.ends_ref, bf16[8,1,192,512]{3,2,1,0:T(8,128)(2,1)} %copy-done.14, bf16[8,1,192,512]{3,2,1,0:T(8,128)(2,1)} %copy-done.14, bf16[8,1,192,512]{3,2,1,0:T(8,128)(2,1)} %copy-done.14), custom_call_target="tpu_custom_call" | custom-call | flops 17179869184 | bytes 4718592 | tf_op jit(solution)/shard_map/attention_forward/pallas_call | solution.py:448
  146.6 13.9 %all-to-all-done.1 = bf16[8,1,64,512]{3,2,1,0:T(8,128)(2,1)S(1)} async-done(((bf16[8,1,64,512]{3,2,1,0:T(8,128)(2,1)}), bf16[8,1,64,512]{3,2,1,0:T(8,128)(2,1)S(1)}, u32[]{:S(2)}, u32[]{:S(2)}) %all-to-all-start.1) | async-done | bytes 524320 | tf_op jit(solution)/shard_map/all_to_all | solution.py:493
  164.3 13.1 %collective-permute-done.5 = bf16[512]{0:T(512)(128)(2,1)S(1)} collective-permute-done((bf16[512]{0:T(512)(128)(2,1)S(1)}, bf16[512]{0:T(512)(128)(2,1)S(1)}, u32[]{:S(2)}, u32[]{:S(2)}) %collective-permute-start.5) | collective-permute-done | bytes 1056 | tf_op jit(solution)/shard_map/ppermute | solution.py:497
  185.7 5.7 fusion.35
  191.3 5.8 multiply_bitcast_fusion
  198.6 7.4 %bitcast_convert_fusion.1 = bf16[512,1024]{1,0:T(8,128)(2,1)S(1)} fusion(bf16[512,2,1312]{0,2,1:T(8,128)(2,1)} %collective-permute-done.2, bf16[512,2,1312]{0,2,1:T(8,128)(2,1)S(1)} %copy-done.33, pred[]{:T(512)S(6)} %eq.29, f32[512,1,1312]{0,2,1:T(8,128)S(1)} %get-tuple-element.89, f32[512,1,1312]{0,2,1:T(8,128)S(1)} %get-tuple-element.85), kind=kOutput, calls=%fused_computation.60 | convolution fusion | flops 2778857472 | bytes 11796481 | tf_op jit(solution)/shard_map/tcf,dcf->td/dot_general | solution.py:617
  223.6 5.7 all-to-all-start.2
  235.8 8.3 %all-to-all-done.2.do_ref = bf16[8,1,64,512]{3,2,1,0:T(8,128)(2,1)} async-done(((bf16[8,1,64,512]{3,2,1,0:T(8,128)(2,1)}), bf16[8,1,64,512]{3,2,1,0:T(8,128)(2,1)}, u32[]{:S(2)}, u32[]{:S(2)}) %all-to-all-start.2) | async-done | bytes 524320 | tf_op jit(solution)/shard_map/all_to_all | solution.py:493
  244.2 51.8 %attention_backward.1 = bf16[8,1,192,512]{3,2,1,0:T(8,128)(2,1)} custom-call(s32[1,4]{1,0:T(1,128)} %reduce_window_sum.18.ends_ref, bf16[8,1,192,512]{3,2,1,0:T(8,128)(2,1)} %copy-done.14, bf16[8,1,192,512]{3,2,1,0:T(8,128)(2,1)} %copy-done.14, bf16[8,1,192,512]{3,2,1,0:T(8,128)(2,1)} %copy-done.14, bf16[8,1,64,512]{3,2,1,0:T(8,128)(2,1)} %all-to-all-done.2.do_ref, ...), custom_call_target="tpu_custom_call" | custom-call | flops 42949672960 | bytes 7864320 | tf_op jit(solution)/shard_map/attention_backward/pallas_call | solution.py:472
  296.0 37.6 %collective-permute-done.11 = bf16[512,512]{1,0:T(8,128)(2,1)} collective-permute-done((bf16[512,512]{1,0:T(8,128)(2,1)}, bf16[512,512]{1,0:T(8,128)(2,1)}, u32[]{:S(2)}, u32[]{:S(2)}) %collective-permute-start.11) | collective-permute-done | bytes 524320 | tf_op jit(solution)/shard_map/ppermute | solution.py:497
  335.9 5.9 add_convert_fusion
  344.7 41.4 %all_to_all.25 = bf16[8,1,192,512]{3,2,1,0:T(8,128)(2,1)S(1)} all-to-all(bf16[8,1,192,512]{3,2,1,0:T(8,128)(2,1)} %attention_backward.1), channel_id=1, replica_groups=mesh['shard'=2,'ctx'=8,'tp'=2] {'ctx'}, dimensions={0} | all-to-all | bytes 3145728 | tf_op jit(solution)/shard_map/all_to_all | solution.py:493
  394.8 6.2 bitcast_convert_fusion
  410.3 30.0 %collective-permute-done.14 = bf16[2,512]{1,0:T(2,128)(2,1)S(1)} collective-permute-done((bf16[2,512]{1,0:T(2,128)(2,1)S(1)}, bf16[2,512]{1,0:T(2,128)(2,1)S(1)}, u32[]{:S(2)}, u32[]{:S(2)}) %collective-permute-start.14) | collective-permute-done | bytes 2080 | tf_op jit(solution)/shard_map/ppermute | solution.py:497
  446.3 5.4 reshape.345
  454.5 4.7 all-to-all-start.4
  482.6 108.5 %all-reduce.6.cloned.1.call-done = (bf16[512,512]{1,0:T(8,128)(2,1)}, bf16[512,2,1312]{0,2,1:T(8,128)(2,1)}, bf16[1312,512]{1,0:T(8,128)(2,1)}) async-done(((bf16[512,512]{1,0:T(8,128)(2,1)}, bf16[512,2,1312]{0,2,1:T(8,128)(2,1)}, bf16[1312,512]{1,0:T(8,128)(2,1)}), (bf16[512,512]{1,0:T(8,128)(2,1)}, bf16[512,2,1312]{0,2,1:T(8,128)(2,1)}, bf16[1312,512]{1,0:T(8,128)(2,1)})) %all-reduce.6.cloned.1.call-update) | async-done | bytes 4554768 | tf_op jit(solution)/shard_map/psum | solution.py:649
  591.0 5.0 convert_element_type.263
  603.2 5.4 collective-permute-done.15
  622.4 5.8 collective-permute-done.21
  633.0 4.9 copy.65
  (200 shorter events, 123.3 us)
Async XLA Ops:
  7.2 8.3 %collective-permute-start.1 = (bf16[512]{0:T(512)(128)(2,1)}, bf16[512]{0:T(512)(128)(2,1)S(1)}, u32[]{:S(2)}, u32[]{:S(2)}) collective-permute-start(bf16[512]{0:T(512)(128)(2,1)} %param.14), channel_id=1, source_target_pairs={{0,16},{16,0},{1,17},{17,1},{2,18},{18,2},{3,19},{19,3},{4,20},{20... | collective-permute-start | bytes 3080 | tf_op jit(solution)/shard_map/ppermute | solution.py:497
  10.2 36.2 %collective-permute-start = (bf16[512,3,512]{2,0,1:T(8,128)(2,1)}, bf16[512,3,512]{2,0,1:T(8,128)(2,1)}, u32[]{:S(2)}, u32[]{:S(2)}) collective-permute-start(bf16[512,3,512]{2,0,1:T(8,128)(2,1)} %param.15), channel_id=1, source_target_pairs={{0,16},{16,0},{1,17},{17,1},{2,18},{18,2},{3,19},{19,3},{4,20},{20... | collective-permute-start | bytes 4718600 | tf_op jit(solution)/shard_map/ppermute | solution.py:497
  52.5 42.0 %all-to-all-start = ((bf16[8,1,192,512]{3,2,1,0:T(8,128)(2,1)}), bf16[8,1,192,512]{3,2,1,0:T(8,128)(2,1)S(1)}, u32[]{:S(2)}, u32[]{:S(2)}) async-start(bf16[8,1,192,512]{3,2,1,0:T(8,128)(2,1)} %bitcast.203), calls=%async_computation | async-start | bytes 3145728 | tf_op jit(solution)/shard_map/all_to_all | solution.py:493
  58.5 83.7 %collective-permute-start.2 = (bf16[512,2,1312]{0,2,1:T(8,128)(2,1)}, bf16[512,2,1312]{0,2,1:T(8,128)(2,1)}, u32[]{:S(2)}, u32[]{:S(2)}) collective-permute-start(bf16[512,2,1312]{0,2,1:T(8,128)(2,1)} %param.18), channel_id=1, source_target_pairs={{0,16},{16,0},{1,17},{17,1},{2,18},{18,2},{3,19},{19,3},{4,20},{20... | collective-permute-start | bytes 8060936 | tf_op jit(solution)/shard_map/ppermute | solution.py:497
  59.8 82.3 %collective-permute-start.3 = (bf16[512,512]{1,0:T(8,128)(2,1)S(1)}, bf16[512,512]{1,0:T(8,128)(2,1)}, u32[]{:S(2)}, u32[]{:S(2)}) collective-permute-start(bf16[512,512]{1,0:T(8,128)(2,1)S(1)} %copy-done.35), channel_id=1, source_target_pairs={{0,16},{16,0},{1,17},{17,1},{2,18},{18,2},{3,19},{19,3},{4,20},{20... | collective-permute-start | bytes 1572872 | tf_op jit(solution)/shard_map/ppermute | solution.py:497
  142.1 18.4 %all-to-all-start.1 = ((bf16[8,1,64,512]{3,2,1,0:T(8,128)(2,1)}), bf16[8,1,64,512]{3,2,1,0:T(8,128)(2,1)S(1)}, u32[]{:S(2)}, u32[]{:S(2)}) async-start(bf16[8,1,64,512]{3,2,1,0:T(8,128)(2,1)} %get-tuple-element.34), calls=%async_computation.1 | async-start | bytes 1048576 | tf_op jit(solution)/shard_map/all_to_all | solution.py:493
  146.1 31.4 %collective-permute-start.6 = (bf16[1312,512]{1,0:T(8,128)(2,1)}, bf16[1312,512]{1,0:T(8,128)(2,1)}, u32[]{:S(2)}, u32[]{:S(2)}) collective-permute-start(bf16[1312,512]{1,0:T(8,128)(2,1)} %param.19), channel_id=1, source_target_pairs={{0,16},{16,0},{1,17},{17,1},{2,18},{18,2},{3,19},{19,3},{4,20},{20... | collective-permute-start | bytes 4030472 | tf_op jit(solution)/shard_map/ppermute | solution.py:497
  163.7 18.1 %collective-permute-start.4 = (bf16[512,1024]{1,0:T(8,128)(2,1)}, bf16[512,1024]{1,0:T(8,128)(2,1)}, u32[]{:S(2)}, u32[]{:S(2)}) collective-permute-start(bf16[512,1024]{1,0:T(8,128)(2,1)} %convolution_convert_fusion.4), channel_id=1, source_target_pairs={{0,1},{1,0},{2,3},{3,2},{4,5},{5,4},{6,7},{7,6},{8,9},{9,8},{10,11... | collective-permute-start | bytes 3145736 | tf_op jit(solution)/shard_map/ppermute | solution.py:497
  163.7 13.7 %collective-permute-start.5 = (bf16[512]{0:T(512)(128)(2,1)S(1)}, bf16[512]{0:T(512)(128)(2,1)S(1)}, u32[]{:S(2)}, u32[]{:S(2)}) collective-permute-start(bf16[512]{0:T(512)(128)(2,1)S(1)} %copy-done.32), channel_id=1, source_target_pairs={{0,16},{16,0},{1,17},{17,1},{2,18},{18,2},{3,19},{19,3},{4,20},{20... | collective-permute-start | bytes 3080 | tf_op jit(solution)/shard_map/ppermute | solution.py:497
  206.1 9.4 %collective-permute-start.8 = (bf16[512,1024]{1,0:T(8,128)(2,1)S(1)}, bf16[512,1024]{1,0:T(8,128)(2,1)S(1)}, u32[]{:S(2)}, u32[]{:S(2)}) collective-permute-start(bf16[512,1024]{1,0:T(8,128)(2,1)S(1)} %bitcast_convert_fusion.1), channel_id=1, source_target_pairs={{0,1},{1,0},{2,3},{3,2},{4,5},{5,4},{6,7},{7,6},{8,9},{9,8},{10,11... | collective-permute-start | bytes 3145736 | tf_op jit(solution)/shard_map/ppermute | solution.py:497
  209.9 6.5 %collective-permute-start.7 = (bf16[512,1024]{1,0:T(8,128)(2,1)S(1)}, bf16[512,1024]{1,0:T(8,128)(2,1)S(1)}, u32[]{:S(2)}, u32[]{:S(2)}) collective-permute-start(bf16[512,1024]{1,0:T(8,128)(2,1)S(1)} %convolution_convert_fusion.3), channel_id=1, source_target_pairs={{0,1},{1,0},{2,3},{3,2},{4,5},{5,4},{6,7},{7,6},{8,9},{9,8},{10,11... | collective-permute-start | bytes 3145736 | tf_op jit(solution)/shard_map/ppermute | solution.py:497
  223.6 20.5 %all-to-all-start.2 = ((bf16[8,1,64,512]{3,2,1,0:T(8,128)(2,1)}), bf16[8,1,64,512]{3,2,1,0:T(8,128)(2,1)}, u32[]{:S(2)}, u32[]{:S(2)}) async-start(bf16[8,1,64,512]{3,2,1,0:T(8,128)(2,1)} %bitcast.208), calls=%async_computation.2 | async-start | bytes 1048576 | tf_op jit(solution)/shard_map/all_to_all | solution.py:493
  229.3 361.7 %all-reduce.6.cloned.1.call-start = ((), (), s32[]{:S(2)}) async-start(), calls=%async_computation.5 | async-start | bytes 9109504 | tf_op jit(solution)/shard_map/psum | solution.py:649
  233.3 100.3 %collective-permute-start.10 = (bf16[512,2,1312]{0,2,1:T(8,128)(2,1)}, bf16[512,2,1312]{0,2,1:T(8,128)(2,1)}, u32[]{:S(2)}, u32[]{:S(2)}) collective-permute-start(bf16[512,2,1312]{0,2,1:T(8,128)(2,1)} %convolution_convert_fusion), channel_id=1, source_target_pairs={{0,16},{16,0},{1,17},{17,1},{2,18},{18,2},{3,19},{19,3},{4,20},{20... | collective-permute-start | bytes 8060936 | tf_op jit(solution)/shard_map/ppermute | solution.py:497
  233.8 99.8 %collective-permute-start.9 = (bf16[1312,512]{1,0:T(8,128)(2,1)}, bf16[1312,512]{1,0:T(8,128)(2,1)}, u32[]{:S(2)}, u32[]{:S(2)}) collective-permute-start(bf16[1312,512]{1,0:T(8,128)(2,1)} %convolution_convert_fusion.1), channel_id=1, source_target_pairs={{0,16},{16,0},{1,17},{17,1},{2,18},{18,2},{3,19},{19,3},{4,20},{20... | collective-permute-start | bytes 4030472 | tf_op jit(solution)/shard_map/ppermute | solution.py:497
  235.3 98.2 %collective-permute-start.11 = (bf16[512,512]{1,0:T(8,128)(2,1)}, bf16[512,512]{1,0:T(8,128)(2,1)}, u32[]{:S(2)}, u32[]{:S(2)}) collective-permute-start(bf16[512,512]{1,0:T(8,128)(2,1)} %convolution_convert_fusion.5), channel_id=1, source_target_pairs={{0,16},{16,0},{1,17},{17,1},{2,18},{18,2},{3,19},{19,3},{4,20},{20... | collective-permute-start | bytes 1572872 | tf_op jit(solution)/shard_map/ppermute | solution.py:497
  403.2 37.2 %collective-permute-start.13 = (bf16[512,3,512]{2,0,1:T(8,128)(2,1)}, bf16[512,3,512]{2,0,1:T(8,128)(2,1)}, u32[]{:S(2)}, u32[]{:S(2)}) collective-permute-start(bf16[512,3,512]{2,0,1:T(8,128)(2,1)} %convolution_convert_fusion.2), channel_id=1, source_target_pairs={{0,16},{16,0},{1,17},{17,1},{2,18},{18,2},{3,19},{19,3},{4,20},{20... | collective-permute-start | bytes 4718600 | tf_op jit(solution)/shard_map/ppermute | solution.py:497
  409.0 31.3 %collective-permute-start.14 = (bf16[2,512]{1,0:T(2,128)(2,1)S(1)}, bf16[2,512]{1,0:T(2,128)(2,1)S(1)}, u32[]{:S(2)}, u32[]{:S(2)}) collective-permute-start(bf16[2,512]{1,0:T(2,128)(2,1)S(1)} %fusion.83), channel_id=1, source_target_pairs={{0,16},{16,0},{1,17},{17,1},{2,18},{18,2},{3,19},{19,3},{4,20},{20... | collective-permute-start | bytes 6152 | tf_op jit(solution)/shard_map/ppermute | solution.py:497
  454.5 144.6 %all-to-all-start.4 = ((bf16[8,80,1536]{2,1,0:T(8,128)(2,1)}), bf16[8,80,1536]{2,1,0:T(8,128)(2,1)}, u32[]{:S(2)}, u32[]{:S(2)}) async-start(bf16[8,80,1536]{2,1,0:T(8,128)(2,1)} %fusion.33), calls=%async_computation.4 | async-start | bytes 3932160 | tf_op jit(solution)/shard_map/all_to_all | solution.py:493
  600.9 7.7 %collective-permute-start.15 = (bf16[80,1536]{1,0:T(8,128)(2,1)S(1)}, bf16[80,1536]{1,0:T(8,128)(2,1)S(1)}, u32[]{:S(2)}, u32[]{:S(2)}) collective-permute-start(bf16[80,1536]{1,0:T(8,128)(2,1)S(1)} %reduce_sum.156), channel_id=1, source_target_pairs={{0,4},{4,8},{8,12},{12,14},{14,10},{10,6},{6,2},{2,0},{1,5},{5,9},... | collective-permute-start | bytes 737288 | tf_op jit(solution)/shard_map/ppermute | solution.py:542
  601.0 7.9 %collective-permute-start.16 = (bf16[80,1536]{1,0:T(8,128)(2,1)S(1)}, bf16[80,1536]{1,0:T(8,128)(2,1)S(1)}, u32[]{:S(2)}, u32[]{:S(2)}) collective-permute-start(bf16[80,1536]{1,0:T(8,128)(2,1)S(1)} %reduce_sum.156), channel_id=1, source_target_pairs={{4,0},{8,4},{12,8},{14,12},{10,14},{6,10},{2,6},{0,2},{5,1},{9,5},... | collective-permute-start | bytes 737288 | tf_op jit(solution)/shard_map/ppermute | solution.py:546
  608.6 6.8 %collective-permute-start.17 = (bf16[80,1536]{1,0:T(8,128)(2,1)S(1)}, bf16[80,1536]{1,0:T(8,128)(2,1)S(1)}, u32[]{:S(2)}, u32[]{:S(2)}) collective-permute-start(bf16[80,1536]{1,0:T(8,128)(2,1)S(1)} %collective-permute-done.15), channel_id=1, source_target_pairs={{0,4},{4,8},{8,12},{12,14},{14,10},{10,6},{6,2},{2,0},{1,5},{5,9},... | collective-permute-start | bytes 737288 | tf_op jit(solution)/shard_map/ppermute | solution.py:542
  608.9 7.1 %collective-permute-start.18 = (bf16[80,1536]{1,0:T(8,128)(2,1)S(1)}, bf16[80,1536]{1,0:T(8,128)(2,1)S(1)}, u32[]{:S(2)}, u32[]{:S(2)}) collective-permute-start(bf16[80,1536]{1,0:T(8,128)(2,1)S(1)} %collective-permute-done.16), channel_id=1, source_target_pairs={{4,0},{8,4},{12,8},{14,12},{10,14},{6,10},{2,6},{0,2},{5,1},{9,5},... | collective-permute-start | bytes 737288 | tf_op jit(solution)/shard_map/ppermute | solution.py:546
  615.4 6.7 %collective-permute-start.19 = (bf16[80,1536]{1,0:T(8,128)(2,1)S(1)}, bf16[80,1536]{1,0:T(8,128)(2,1)S(1)}, u32[]{:S(2)}, u32[]{:S(2)}) collective-permute-start(bf16[80,1536]{1,0:T(8,128)(2,1)S(1)} %collective-permute-done.17), channel_id=1, source_target_pairs={{0,4},{4,8},{8,12},{12,14},{14,10},{10,6},{6,2},{2,0},{1,5},{5,9},... | collective-permute-start | bytes 737288 | tf_op jit(solution)/shard_map/ppermute | solution.py:542
  (42 other events, 637.1 us)
Sparse Core Ops, SparseCore 0:
  403.9 187.1 all-reduce.5
